TPU v7x, 512 devices: a whole 4x4x16 slice. The times are simulated.
512 devices in a mesh: pp: 16 (over y, x), ep: 32 (over z, core).
Axes of the slice: x: 4, y: 4, z: 16, core: 2. Of those that a mesh axis runs over, the one named last changes fastest.
Arguments:
- upstream: bfloat16 [16, 4096, 3584], P('pp', 'ep'), may hold values from -0.375 to 0.375
- routes: int32 [16, 4096, 2], P('pp', 'ep'), may hold values from 0 to 3, all different within a row; in each aligned block of 128 rows (0 to 127, 128 to 255, ..., all dimensions but the last counted through in order) at most 120 rows name the same one
- gates: float32 [16, 4096, 2], P('pp', 'ep'), may hold values from 0.1 to 1.2
- hidden_saved: bfloat16 [16, 32, 960, 512], P('pp', 'ep'), may hold values from -6 to 6
- down_weight: bfloat16 [16, 32, 512, 896], P('pp', 'ep'), as said below
- first_moment: bfloat16 [16, 32, 256, 896], P('pp', 'ep'), may hold values from -1.796875 to 1.796875
- second_moment: bfloat16 [16, 32, 256, 896], P('pp', 'ep'), may hold values from 0.25 to 4
Outputs:
- gate_grad: float32 [16, 4096, 2], P('pp', 'ep')
- new_weight: bfloat16 [16, 32, 256, 896], P('pp', 'ep')
- new_first: bfloat16 [16, 32, 256, 896], P('pp', 'ep')
- new_second: bfloat16 [16, 32, 256, 896], P('pp', 'ep')
Inputs may be any that keep to these rules, and one draw needn't show every extreme that they name: `routes`: each row names 2 different experts. Within the rows of one device no expert is named more than 120 times, a bound that some block reaches. down_weight[i] equals down_weight[15 - i]: a rank and its mirror hold the same section.
All inputs are finite; a program needn't handle non-finite values.
Results may differ from a plain program's by a relative error of at most 0.005.
Values may be sent and summed in bfloat16 or wider, within the bound.
No kernel may reach another device: no remote copies, remote signals or barrier semaphores. Data moves between devices by JAX's collectives and lax.ppermute only.
A program may use at most 128 MiB of HBM per device.

v0:
```python
import jax
import jax.numpy as jnp
from jax import lax
from jax.sharding import PartitionSpec as P

EXP = 4
TOP = 2
SPLITS = 2
CAP = 120


beta_first = 0.9
beta_second = 0.95
learn_rate = 0.00022
decay_rate = 0.1
epsilon = 1e-08
step_count = 10


def from_partner(block, axis, distance):
    count = lax.axis_size(axis)
    route = []
    for low in range(count):
        high = low | 1 << distance
        if high != low and high < count:
            route += [(low, high), (high, low)]
    return lax.ppermute(block, axis, route)


def slot_numbers(route_rows):
    flat_routes = route_rows.reshape(-1)
    onehot = (flat_routes[:, None] == jnp.arange(EXP, dtype=jnp.int32)[None, :]).astype(jnp.int32)
    before = jnp.cumsum(onehot, axis=0) - onehot
    return jnp.sum(before * onehot, axis=1)


def block_size(row_total):
    block_rows = row_total
    while block_rows > 1024 and block_rows % 2 == 0:
        block_rows = block_rows // 2
    return block_rows


def shards(upstream, routes, gates, hidden_saved, down_weight, first_moment, second_moment):
    rows_in = upstream[0]
    route_dev = routes[0]
    gate_dev = gates[0]
    tokens = rows_in.shape[0]
    row_width = rows_in.shape[1]
    device_count = lax.axis_size("ep")
    groups = device_count // EXP
    feat_count = groups // SPLITS
    feature_part = row_width // feat_count
    feat_bits = feat_count.bit_length() - 1
    position = lax.axis_index("ep")
    slot_index = slot_numbers(route_dev)
    target = route_dev.reshape(-1) * CAP + slot_index
    assign_count = tokens * TOP
    inverse = (
        jnp.full((EXP * CAP,), assign_count, jnp.int32)
        .at[target]
        .set(jnp.arange(assign_count, dtype=jnp.int32))
    )
    scaled = (gate_dev[:, :, None] * rows_in[:, None, :].astype(jnp.float32)).astype(jnp.bfloat16)
    padded = jnp.concatenate(
        [scaled.reshape(assign_count, row_width), jnp.zeros((1, row_width), jnp.bfloat16)], axis=0
    )
    slotted = jnp.take(padded, inverse, axis=0).reshape(EXP, CAP, feat_count, feature_part)
    hidden = hidden_saved[0, 0]
    for level in range(feat_bits):
        partner_rows = from_partner(hidden, "ep", level)
        level_bit = position >> level & 1
        hidden = jnp.where(
            level_bit == 0,
            jnp.concatenate([hidden, partner_rows], axis=0),
            jnp.concatenate([partner_rows, hidden], axis=0),
        )
    weight = down_weight[0, 0]
    unit_count = weight.shape[0]
    row_total = hidden.shape[0]
    outgoing = jnp.broadcast_to(
        slotted.transpose(0, 2, 1, 3)[:, None], (EXP, SPLITS, feat_count, CAP, feature_part)
    )
    outgoing = outgoing.reshape(device_count, CAP, feature_part)
    expert_rows = lax.all_to_all(outgoing, "ep", split_axis=0, concat_axis=0, tiled=True).reshape(
        row_total, feature_part
    )
    block_rows = block_size(row_total)

    def block_dots(operands):
        part_hidden, part_rows = operands
        output = jnp.dot(part_hidden, weight, preferred_element_type=jnp.float32)
        return jnp.sum(part_rows.astype(jnp.float32) * output, axis=1)

    row_dots = lax.map(
        block_dots,
        (
            hidden.reshape(-1, block_rows, unit_count),
            expert_rows.reshape(-1, block_rows, feature_part),
        ),
    ).reshape(row_total)
    row_dots = row_dots.reshape(device_count, CAP)
    weight_grad = lax.dot_general(
        hidden, expert_rows, (((0,), (0,)), ((), ())), preferred_element_type=jnp.float32
    )
    returned = lax.all_to_all(row_dots, "ep", split_axis=0, concat_axis=0, tiled=True)
    totals = jnp.sum(returned.reshape(EXP, groups, CAP), axis=1).reshape(-1)
    gate_grad = jnp.take(totals, target).reshape(tokens, TOP) / gate_dev
    pipe_rank = lax.axis_index("pp")
    rank_count = lax.axis_size("pp")
    lower_rank = pipe_rank < rank_count // 2
    half_units = unit_count // 2
    grad_round = weight_grad.astype(jnp.bfloat16)
    kept_rows = jnp.where(lower_rank, grad_round[:half_units], grad_round[half_units:])
    moving = jnp.where(lower_rank, grad_round[half_units:], grad_round[:half_units])
    bit_order = list(range(rank_count.bit_length() - 1))
    for bit_place in bit_order:
        moving = from_partner(moving, "pp", bit_place)
    summed = kept_rows.astype(jnp.float32) + moving.astype(jnp.float32)
    weight_kept = jnp.where(lower_rank, weight[:half_units], weight[half_units:]).astype(
        jnp.float32
    )
    first_new = beta_first * first_moment[0, 0].astype(jnp.float32) + (1.0 - beta_first) * summed
    second_new = (
        beta_second * second_moment[0, 0].astype(jnp.float32)
        + (1.0 - beta_second) * summed * summed
    )
    first_hat = first_new / (1.0 - beta_first**step_count)
    second_hat = second_new / (1.0 - beta_second**step_count)
    new_weight = weight_kept - learn_rate * (
        first_hat / (jnp.sqrt(second_hat) + epsilon) + decay_rate * weight_kept
    )
    return (
        gate_grad[None],
        new_weight.astype(jnp.bfloat16)[None, None],
        first_new.astype(jnp.bfloat16)[None, None],
        second_new.astype(jnp.bfloat16)[None, None],
    )


def solution(mesh):
    placed = (
        P("pp", "ep", None),
        P("pp", "ep", None),
        P("pp", "ep", None),
        P("pp", "ep", None, None),
        P("pp", "ep", None, None),
        P("pp", "ep", None, None),
        P("pp", "ep", None, None),
    )
    return jax.shard_map(
        shards,
        mesh=mesh,
        in_specs=placed,
        out_specs=(
            P("pp", "ep", None),
            P("pp", "ep", None, None),
            P("pp", "ep", None, None),
            P("pp", "ep", None, None),
        ),
        check_vma=False,
    )
```

profile of v0, /device:TPU:1, one launch (start us, length us, event | category | flops | bytes accessed | tf_op | source)
XLA Modules:
  0.0 492.6 jit_solution(3187953648421723870)
XLA Ops:
  7.3 3.0 mul.89
  10.3 5.7 %mul.90 = f32[256,3584]{1,0:T(8,128)} reshape(f32[128,2,3584]{2,1,0:T(2,128)} %mul.89) | data formatting | bytes 7340032 | tf_op jit(solution)/shard_map/mul | solution.py:64
  18.5 4.1 gather_fusion
  22.6 3.9 gather.13
  29.0 3.5 broadcast_in_dim.55
  32.4 16.9 %all-to-all-start = ((bf16[32,120,896]{2,1,0:T(8,128)(2,1)}), bf16[32,120,896]{2,1,0:T(8,128)(2,1)}, u32[]{:S(2)}, u32[]{:S(2)}) async-start(bf16[32,120,896]{2,1,0:T(8,128)(2,1)} %bitcast.82), calls=%async_computation | async-start | bytes 13762560 | tf_op jit(solution)/shard_map/all_to_all | solution.py:85
  56.1 3.5 collective-permute-start.1
  59.6 329.1 %collective-permute-done.1 = bf16[1920,512]{1,0:T(8,128)(2,1)} collective-permute-done((bf16[1920,512]{1,0:T(8,128)(2,1)S(1)}, bf16[1920,512]{1,0:T(8,128)(2,1)}, u32[]{:S(2)}, u32[]{:S(2)}) %collective-permute-start.1) | collective-permute-done | bytes 1966112 | tf_op jit(solution)/shard_map/ppermute | solution.py:27
  388.7 4.0 maximum_select_fusion
  392.7 8.4 %convolution_convert_fusion = bf16[512,896]{1,0:T(8,128)(2,1)S(1)} fusion(bf16[3840,512]{1,0:T(8,128)(2,1)} %maximum_select_fusion, bf16[3840,896]{1,0:T(8,128)(2,1)} %bitcast.17), kind=kOutput, calls=%fused_computation.12 | convolution fusion | flops 3523674112 | bytes 11730944 | tf_op jit(solution)/shard_map/dot_general | solution.py:103
  401.2 3.1 collective-permute-start.2
  404.4 9.9 %collective-permute-done.2 = bf16[256,896]{1,0:T(8,128)(2,1)S(1)} collective-permute-done((bf16[256,896]{1,0:T(8,128)(2,1)S(1)}, bf16[256,896]{1,0:T(8,128)(2,1)S(1)}, u32[]{:S(2)}, u32[]{:S(2)}) %collective-permute-start.2) | collective-permute-done | bytes 458784 | tf_op jit(solution)/shard_map/ppermute | solution.py:27
  414.3 4.6 collective-permute-start.3
  418.9 9.0 %collective-permute-done.3 = bf16[256,896]{1,0:T(8,128)(2,1)S(1)} collective-permute-done((bf16[256,896]{1,0:T(8,128)(2,1)S(1)}, bf16[256,896]{1,0:T(8,128)(2,1)S(1)}, u32[]{:S(2)}, u32[]{:S(2)}) %collective-permute-start.3) | collective-permute-done | bytes 458784 | tf_op jit(solution)/shard_map/ppermute | solution.py:27
  427.9 3.2 collective-permute-start.4
  431.3 8.0 %collective-permute-done.4 = bf16[256,896]{1,0:T(8,128)(2,1)} collective-permute-done((bf16[256,896]{1,0:T(8,128)(2,1)S(1)}, bf16[256,896]{1,0:T(8,128)(2,1)}, u32[]{:S(2)}, u32[]{:S(2)}) %collective-permute-start.4) | collective-permute-done | bytes 458784 | tf_op jit(solution)/shard_map/ppermute | solution.py:27
  439.2 4.8 collective-permute-start.5
  444.1 12.7 %while.10 = (s32[]{:T(128)}, f32[4,960]{1,0:T(4,128)S(1)}, bf16[4,960,896]{2,1,0:T(8,128)(2,1)}, bf16[4,960,512]{2,1,0:T(8,128)(2,1)}, bf16[512,896]{1,0:T(8,128)(2,1)S(1)}, /*index=5*/s32[]{:T(128)}, s32[]{:T(128)}) while((s32[]{:T(128)}, f32[4,960]{1,0:T(4,128)S(1)}, bf16[4,960,896]{2,1,0:T(8,128)(2,1)}, bf16[4,960,512]{2,1,0:T(8,128)(2,1)}, ...), condition=%wide.region_6.7_spmd, body=%wide.region_4.6_spmd.sunk | while | flops 883383360 | bytes 3633489 | solution.py:95
  444.1 3.1 fusion.24
  447.3 3.1 fusion.24
  450.4 3.0 fusion.24
  453.6 3.1 fusion.24
  457.5 16.0 %all-to-all-start.1 = ((f32[32,1,120]{2,1,0:T(1,128)}), f32[32,1,120]{2,1,0:T(1,128)S(1)}, u32[]{:S(2)}, u32[]{:S(2)}) async-start(f32[32,1,120]{2,1,0:T(1,128)} %all_to_all.10), calls=%async_computation.1 | async-start | bytes 32768 | tf_op jit(solution)/shard_map/all_to_all | solution.py:106
  473.5 11.7 %all-to-all-done.1 = f32[32,1,120]{2,1,0:T(1,128)S(1)} async-done(((f32[32,1,120]{2,1,0:T(1,128)}), f32[32,1,120]{2,1,0:T(1,128)S(1)}, u32[]{:S(2)}, u32[]{:S(2)}) %all-to-all-start.1) | async-done | bytes 15392 | tf_op jit(solution)/shard_map/all_to_all | solution.py:106
  (62 shorter events, 26.9 us)
Async XLA Ops:
  5.8 4.6 copy-start.3
  32.4 16.9 %copy-start.1 = (bf16[1,1,960,512]{3,2,1,0:T(8,128)(2,1)S(1)}, bf16[1,1,960,512]{3,2,1,0:T(8,128)(2,1)}, u32[]{:S(2)}) copy-start(bf16[1,1,960,512]{3,2,1,0:T(8,128)(2,1)} %param.12) | copy-start | bytes 2949124
  32.4 360.3 %all-to-all-start = ((bf16[32,120,896]{2,1,0:T(8,128)(2,1)}), bf16[32,120,896]{2,1,0:T(8,128)(2,1)}, u32[]{:S(2)}, u32[]{:S(2)}) async-start(bf16[32,120,896]{2,1,0:T(8,128)(2,1)} %bitcast.82), calls=%async_computation | async-start | bytes 13762560 | tf_op jit(solution)/shard_map/all_to_all | solution.py:85
  49.4 4.6 collective-permute-start
  56.1 332.6 %collective-permute-start.1 = (bf16[1920,512]{1,0:T(8,128)(2,1)S(1)}, bf16[1920,512]{1,0:T(8,128)(2,1)}, u32[]{:S(2)}, u32[]{:S(2)}) collective-permute-start(bf16[1920,512]{1,0:T(8,128)(2,1)S(1)} %maximum_select_fusion.1), channel_id=1, source_target_pairs={{0,2},{2,0},{1,3},{3,1},{4,6},{6,4},{5,7},{7,5},{8,10},{10,8},{9,1... | collective-permute-start | bytes 5898248 | tf_op jit(solution)/shard_map/ppermute | solution.py:27
  392.7 51.3 %copy-start.2 = (bf16[1,1,512,896]{3,2,1,0:T(8,128)(2,1)S(1)}, bf16[1,1,512,896]{3,2,1,0:T(8,128)(2,1)}, u32[]{:S(2)}) copy-start(bf16[1,1,512,896]{3,2,1,0:T(8,128)(2,1)} %param.13) | copy-start | bytes 2752516
  401.2 13.1 %collective-permute-start.2 = (bf16[256,896]{1,0:T(8,128)(2,1)S(1)}, bf16[256,896]{1,0:T(8,128)(2,1)S(1)}, u32[]{:S(2)}, u32[]{:S(2)}) collective-permute-start(bf16[256,896]{1,0:T(8,128)(2,1)S(1)} %broadcast_select_fusion), channel_id=1, source_target_pairs={{0,32},{32,0},{64,96},{96,64},{128,160},{160,128},{192,224},{224,1... | collective-permute-start | bytes 1376264 | tf_op jit(solution)/shard_map/ppermute | solution.py:27
  414.3 13.6 %collective-permute-start.3 = (bf16[256,896]{1,0:T(8,128)(2,1)S(1)}, bf16[256,896]{1,0:T(8,128)(2,1)S(1)}, u32[]{:S(2)}, u32[]{:S(2)}) collective-permute-start(bf16[256,896]{1,0:T(8,128)(2,1)S(1)} %collective-permute-done.2), channel_id=1, source_target_pairs={{0,64},{64,0},{32,96},{96,32},{128,192},{192,128},{160,224},{224,1... | collective-permute-start | bytes 1376264 | tf_op jit(solution)/shard_map/ppermute | solution.py:27
  427.9 11.3 %collective-permute-start.4 = (bf16[256,896]{1,0:T(8,128)(2,1)S(1)}, bf16[256,896]{1,0:T(8,128)(2,1)}, u32[]{:S(2)}, u32[]{:S(2)}) collective-permute-start(bf16[256,896]{1,0:T(8,128)(2,1)S(1)} %collective-permute-done.3), channel_id=1, source_target_pairs={{0,128},{128,0},{32,160},{160,32},{64,192},{192,64},{96,224},{224,... | collective-permute-start | bytes 1376264 | tf_op jit(solution)/shard_map/ppermute | solution.py:27
  439.2 50.3 %collective-permute-start.5 = (bf16[256,896]{1,0:T(8,128)(2,1)}, bf16[256,896]{1,0:T(8,128)(2,1)S(1)}, u32[]{:S(2)}, u32[]{:S(2)}) collective-permute-start(bf16[256,896]{1,0:T(8,128)(2,1)} %collective-permute-done.4), channel_id=1, source_target_pairs={{0,256},{256,0},{32,288},{288,32},{64,320},{320,64},{96,352},{352,... | collective-permute-start | bytes 1376264 | tf_op jit(solution)/shard_map/ppermute | solution.py:27
  444.0 43.3 %copy-start.4 = (f32[1,128,2]{2,1,0:T(8,128)S(1)}, f32[1,128,2]{2,1,0:T(8,128)}, u32[]{:S(2)}) copy-start(f32[1,128,2]{2,1,0:T(8,128)} %copy-done.3) | copy-start | bytes 3076
  444.1 45.5 %copy-start = (bf16[1,1,256,896]{3,2,1,0:T(8,128)(2,1)S(1)}, bf16[1,1,256,896]{3,2,1,0:T(8,128)(2,1)}, u32[]{:S(2)}) copy-start(bf16[1,1,256,896]{3,2,1,0:T(8,128)(2,1)} %param.15) | copy-start | bytes 1376260
  456.7 33.9 %copy-start.5 = (bf16[1,1,256,896]{3,2,1,0:T(8,128)(2,1)S(1)}, bf16[1,1,256,896]{3,2,1,0:T(8,128)(2,1)}, u32[]{:S(2)}) copy-start(bf16[1,1,256,896]{3,2,1,0:T(8,128)(2,1)} %param.14) | copy-start | bytes 1376260
  457.5 27.7 %all-to-all-start.1 = ((f32[32,1,120]{2,1,0:T(1,128)}), f32[32,1,120]{2,1,0:T(1,128)S(1)}, u32[]{:S(2)}, u32[]{:S(2)}) async-start(f32[32,1,120]{2,1,0:T(1,128)} %all_to_all.10), calls=%async_computation.1 | async-start | bytes 32768 | tf_op jit(solution)/shard_map/all_to_all | solution.py:106
where the time goes:
time: 493 us
  waiting for transfers between devices  370 us (75%)
  starting transfers between devices  54.4 us (11%)
  local copies, waits for them, and re-layouts  29.3 us (6%)
  matrix products  20.7 us (4%)
  other arithmetic  17 us (3%)
    ppermute x6, waiting for transfers between devices, from_partner(): return lax.ppermute(block, axis, route)  358 us
    ppermute x6, starting transfers between devices, from_partner(): return lax.ppermute(block, axis, route)  21.5 us
    all_to_all x1, starting transfers between devices, shards(): lax.all_to_all(outgoing, 'ep', split_axis=0, concat_axis=0, tiled=True)  16.9 us
    all_to_all x1, starting transfers between devices, shards(): lax.all_to_all(row_dots, 'ep', split_axis=0, concat_axis=0, tiled=True)  16 us
    dot_general x4, matrix products, block_dots(): output = jnp.dot(part_hidden, weight, preferred_element_type=jnp.float32)  12.3 us
    all_to_all x1, waiting for transfers between devices, shards(): lax.all_to_all(row_dots, 'ep', split_axis=0, concat_axis=0, tiled=True)  11.7 us
  transfers between devices with their start and end apart: 8, of which 6 were waited for; matrix products, arithmetic and copies ran while one was open for 5% of the time, Pallas kernels for 0%

commit v1 on v0

v1 whole, which is shorter than its diff:
```python
import jax
import jax.numpy as jnp
from jax import lax
from jax.experimental import pallas as pl
from jax.experimental.pallas import tpu as pltpu
from jax.sharding import PartitionSpec as P

EXP = 4
TOP = 2
SPLITS = 2
CAP = 120

beta_first = 0.9
beta_second = 0.95
learn_rate = 0.00022
decay_rate = 0.1
epsilon = 1e-08
step_count = 10

VMEM_BYTES = 40 * 1024 * 1024

OFFSETS = (0, -1, 1, -2, 2, -3, 3, -4, 4, -5, 5, -6, 6, -7, 7, 8)
ROUNDS = ((0, 5), (5, 9), (9, 13), (13, 16))


def send_chips(block, hops):
    count = lax.axis_size("ep")
    return lax.ppermute(block, "ep", [(i, (i + 2 * hops) % count) for i in range(count)])


def swap_bits(block, bits):
    count = lax.axis_size("ep")
    return lax.ppermute(block, "ep", [(i, i ^ bits) for i in range(count)])


def place_kernel(index, meta, rows, out):
    expert, core = index[16], index[17]
    tokens = meta.shape[2]
    lower = lax.broadcasted_iota(jnp.int32, (tokens, tokens), 0) > lax.broadcasted_iota(
        jnp.int32, (tokens, tokens), 1
    )
    lower = lower.astype(jnp.float32).astype(jnp.bfloat16)
    slots = rows.shape[0]
    lane = lax.broadcasted_iota(jnp.int32, (tokens, slots), 1).astype(jnp.float32)
    wanted = expert.astype(jnp.float32)
    for half in range(2):
        owner = core if half == 0 else 1 - core
        table = jnp.transpose(meta[owner])
        first = table[:, 0:1] == wanted
        second = table[:, 1:2] == wanted
        named = jnp.where(first | second, 1.0, 0.0)
        gate = jnp.where(first, table[:, 2:3], 0.0) + jnp.where(second, table[:, 3:4], 0.0)
        wide = jnp.broadcast_to(named, (tokens, slots))
        before = jnp.dot(lower, wide.astype(jnp.bfloat16), preferred_element_type=jnp.float32)
        place = before + (owner * CAP).astype(jnp.float32)
        onehot = jnp.where(place == lane, wide, 0.0).astype(jnp.bfloat16)
        picked = jnp.dot(onehot, rows[...], preferred_element_type=jnp.float32)
        out[0, half * tokens : (half + 1) * tokens, :] = (gate * picked).astype(out.dtype)


def place_rows(index, meta, hidden):
    tokens = meta.shape[2]
    units = hidden.shape[1]
    return pl.pallas_call(
        place_kernel,
        grid_spec=pltpu.PrefetchScalarGridSpec(
            num_scalar_prefetch=1,
            grid=(16,),
            in_specs=[
                pl.BlockSpec((2, 8, tokens), lambda i, ix: (ix[i], 0, 0)),
                pl.BlockSpec((2 * CAP, units), lambda i, ix: (ix[18 + i], 0)),
            ],
            out_specs=pl.BlockSpec((1, 2 * tokens, units), lambda i, ix: (i, 0, 0)),
        ),
        out_shape=jax.ShapeDtypeStruct((16, 2 * tokens, units), jnp.bfloat16),
        cost_estimate=pl.CostEstimate(
            flops=2 * 16 * 256 * 240 * (units + 128), bytes_accessed=16 * 512 * units * 2, transcendentals=0
        ),
        compiler_params=pltpu.CompilerParams(vmem_limit_bytes=VMEM_BYTES),
        name="place_rows",
    )(index, meta, hidden)


def block_dots(index, start, rows, hidden, weight, dots):
    for b, part in enumerate(rows):
        output = jnp.dot(hidden[b], weight[...], preferred_element_type=jnp.float32)
        column = jnp.sum(part[...].astype(jnp.float32) * output, axis=1, keepdims=True)
        line = jnp.transpose(jnp.broadcast_to(column, (column.shape[0], 128)))[0:1]
        for half in range(2):
            owner = index[34 + 2 * (start + b) + half]
            dots[pl.ds(owner, 1)] = line[:, half * 128 : (half + 1) * 128].reshape(1, 1, 128)


def add_grads(rows, hidden, before, after):
    total = None if before is None else before[...]
    for b, part in enumerate(rows):
        term = lax.dot_general(
            hidden[b], part[...], (((0,), (0,)), ((), ())), preferred_element_type=jnp.float32
        )
        total = term if total is None else total + term
    after[...] = total.astype(after.dtype)


def round_call(index, start, rows, placed, weight, grads, dots):
    count = len(rows)
    units, width = weight.shape
    tokens = rows[0].shape[0]
    first = grads is None

    def kernel(ix, hid, wgt, *refs):
        parts, refs = refs[:count], refs[count:]
        if first:
            grads_out, dots_out = refs
            dots_out[...] = jnp.zeros_like(dots_out)
            grads_in = None
        else:
            grads_in, dots_in, grads_out, dots_out = refs
            dots_out[...] = dots_in[...]
        block_dots(ix, start, parts, hid, wgt, dots_out)
        add_grads(parts, hid, grads_in, grads_out)

    whole = lambda shape: pl.BlockSpec(shape, lambda i, ix: (0,) * len(shape))
    hid_spec = pl.BlockSpec((count, tokens, units), lambda i, ix: (0, 0, 0))
    in_specs = [hid_spec, whole(weight.shape)] + [whole(rows[0].shape)] * count
    operands = [placed, weight, *rows]
    aliases = {}
    if not first:
        in_specs += [whole((units, width)), whole((32, 1, 128))]
        operands += [grads, dots]
        aliases = {count + 3: 0, count + 4: 1}
    return pl.pallas_call(
        kernel,
        grid_spec=pltpu.PrefetchScalarGridSpec(
            num_scalar_prefetch=1,
            grid=(1,),
            in_specs=in_specs,
            out_specs=[whole((units, width)), whole((32, 1, 128))],
        ),
        out_shape=[
            jax.ShapeDtypeStruct((units, width), jnp.float32),
            jax.ShapeDtypeStruct((32, 1, 128), jnp.float32),
        ],
        input_output_aliases=aliases,
        cost_estimate=pl.CostEstimate(
            flops=4 * count * tokens * units * width,
            bytes_accessed=8 * units * width + count * tokens * (units + width) * 2,
            transcendentals=0,
        ),
        compiler_params=pltpu.CompilerParams(vmem_limit_bytes=VMEM_BYTES),
        name="round_blocks",
    )(index, *operands)


def last_dots(index, start, rows, placed, weight, dots):
    count = len(rows)
    tokens = rows[0].shape[0]

    def kernel(ix, hid, wgt, *refs):
        parts, (dots_in, dots_out) = refs[:count], refs[count:]
        dots_out[...] = dots_in[...]
        block_dots(ix, start, parts, hid, wgt, dots_out)

    whole = lambda shape: pl.BlockSpec(shape, lambda i, ix: (0,) * len(shape))
    return pl.pallas_call(
        kernel,
        grid_spec=pltpu.PrefetchScalarGridSpec(
            num_scalar_prefetch=1,
            grid=(1,),
            in_specs=[whole(placed.shape), whole(weight.shape)]
            + [whole(rows[0].shape)] * count
            + [whole((32, 1, 128))],
            out_specs=whole((32, 1, 128)),
        ),
        out_shape=jax.ShapeDtypeStruct((32, 1, 128), jnp.float32),
        input_output_aliases={count + 3: 0},
        cost_estimate=pl.CostEstimate(
            flops=2 * count * tokens * weight.size, bytes_accessed=2 * weight.size, transcendentals=0
        ),
        compiler_params=pltpu.CompilerParams(vmem_limit_bytes=VMEM_BYTES),
        name="last_dots",
    )(index, *([placed, weight, *rows, dots]))


def last_grads(which, rows, placed, grads):
    count = len(rows)
    tokens = rows[0].shape[0]
    units, width = grads.shape
    half = units // 2

    def kernel(ix, hid, grads_in, *refs):
        parts, (out,) = refs[:count], refs[count:]
        add_grads(parts, hid, grads_in, out)

    whole = lambda shape: pl.BlockSpec(shape, lambda i, ix: (0,) * len(shape))
    return pl.pallas_call(
        kernel,
        grid_spec=pltpu.PrefetchScalarGridSpec(
            num_scalar_prefetch=1,
            grid=(1,),
            in_specs=[
                pl.BlockSpec((count, tokens, half), lambda i, ix: (0, 0, ix[0])),
                pl.BlockSpec((half, width), lambda i, ix: (ix[0], 0)),
            ]
            + [whole(rows[0].shape)] * count,
            out_specs=whole((half, width)),
        ),
        out_shape=jax.ShapeDtypeStruct((half, width), jnp.bfloat16),
        cost_estimate=pl.CostEstimate(
            flops=2 * count * tokens * half * width, bytes_accessed=6 * half * width, transcendentals=0
        ),
        compiler_params=pltpu.CompilerParams(vmem_limit_bytes=VMEM_BYTES),
        name="last_grads",
    )(which, placed, grads, *rows)


def shards(upstream, routes, gates, hidden_saved, down_weight, first_moment, second_moment):
    rows_in = upstream[0]
    route_dev = routes[0]
    gate_dev = gates[0]
    weight = down_weight[0, 0]
    tokens, row_width = rows_in.shape
    units, part = weight.shape
    position = lax.axis_index("ep")
    chip, core = position // 2, position % 2
    parity = chip % 2
    expert, block = position // 8, position % 4

    source = (chip + jnp.array(OFFSETS, jnp.int32)) % 16
    hidden_at = ((source // 4) ^ block) * 4 + source % 4
    owners = (2 * source[:, None] + (core ^ jnp.arange(2, dtype=jnp.int32))[None, :]).reshape(-1)
    index = jnp.concatenate([source, jnp.stack([expert, core]), hidden_at, owners]).astype(jnp.int32)

    def features(at):
        return lax.dynamic_slice(rows_in, (0, at * part), (tokens, part))

    outgoing = jnp.stack([features(block ^ 1), features(block ^ 3)])
    incoming = swap_bits(outgoing, 1)
    same = jnp.concatenate([features(block), incoming[0]], axis=0)
    diff = jnp.concatenate([features(block ^ 2), incoming[1]], axis=0)

    own_hidden = hidden_saved[0, 0]
    chip_hidden = swap_bits(own_hidden, 2)
    meta = jnp.concatenate([route_dev.astype(jnp.float32), gate_dev], axis=1)
    meta = jnp.pad(meta.T, ((0, 4), (0, 0)))
    meta = jnp.broadcast_to(meta[None], (lax.axis_size("ep"),) + meta.shape)

    diff_steps = [(send_chips(diff, 1), send_chips(diff, -1))]
    same_steps = [(send_chips(same, 2), send_chips(same, -2))]
    grads = dots = placed = None
    for step in range(1, 4):
        ahead = diff_steps[-1] if step == 1 else diff_steps[-1] + same_steps[-2]
        if step == 3:
            ahead = ahead + (placed,)
        ahead = lax.optimization_barrier(ahead)
        diff_steps.append((send_chips(ahead[0], 2), send_chips(ahead[1], -2)))
        ahead = same_steps[-1] + diff_steps[-2]
        if step == 3:
            ahead = ahead + (grads,)
        ahead = lax.optimization_barrier(ahead)
        if step == 1:
            meta = lax.optimization_barrier((meta,) + ahead[:2])[0]
            meta = lax.all_to_all(meta, "ep", split_axis=0, concat_axis=0, tiled=True)
            hidden = jnp.concatenate(
                [own_hidden, swap_bits(own_hidden, 1), chip_hidden, swap_bits(chip_hidden, 1)],
                axis=0,
            )
            placed = place_rows(index, meta, hidden)
        if step < 3:
            same_steps.append((send_chips(ahead[0], 2), send_chips(ahead[1], -2)))
        else:
            across = jnp.concatenate(
                [send_chips(ahead[0][:tokens], 2), send_chips(ahead[1][tokens:], -2)], axis=0
            )
        if step > 1:
            start, stop = ROUNDS[step - 2]
            rows = list(diff_steps[step - 2] + same_steps[step - 2])
            rows = [same] + rows if step == 2 else rows
            grads, dots = round_call(index, start, rows, placed[start:stop], weight, grads, dots)
    start, stop = ROUNDS[2]
    rows = list(diff_steps[2] + same_steps[2])
    grads, dots = round_call(index, start, rows, placed[start:stop], weight, grads, dots)
    far_forth, far_back = diff_steps[3]
    last = [far_forth, far_back, across]
    start, stop = ROUNDS[3]
    placed_last = placed[start:stop]

    pipe_rank = lax.axis_index("pp")
    rank_count = lax.axis_size("pp")
    upper = (pipe_rank >= rank_count // 2).astype(jnp.int32)
    half_units = units // 2
    moving = last_grads(jnp.stack([1 - upper]), last, placed_last, grads)
    moving = lax.ppermute(moving, "pp", [(i, rank_count - 1 - i) for i in range(rank_count)])
    dots = last_dots(index, start, last, placed_last, weight, dots)
    returned = lax.all_to_all(dots, "ep", split_axis=0, concat_axis=0, tiled=True)
    kept = last_grads(jnp.stack([upper]), last, placed_last, grads)

    summed = kept.astype(jnp.float32) + moving.astype(jnp.float32)
    weight_kept = lax.dynamic_slice(weight, (upper * half_units, 0), (half_units, part)).astype(
        jnp.float32
    )
    first_new = beta_first * first_moment[0, 0].astype(jnp.float32) + (1.0 - beta_first) * summed
    second_new = (
        beta_second * second_moment[0, 0].astype(jnp.float32)
        + (1.0 - beta_second) * summed * summed
    )
    first_hat = first_new / (1.0 - beta_first**step_count)
    second_hat = second_new / (1.0 - beta_second**step_count)
    new_weight = weight_kept - learn_rate * (
        first_hat / (jnp.sqrt(second_hat) + epsilon) + decay_rate * weight_kept
    )

    totals = jnp.sum(returned.reshape(EXP, 8, tokens), axis=1)
    named = route_dev[:, :, None] == jnp.arange(EXP, dtype=jnp.int32)[None, None, :]
    gate_grad = jnp.sum(jnp.where(named, totals.T[:, None, :], 0.0), axis=2) / gate_dev
    return (
        gate_grad[None],
        new_weight.astype(jnp.bfloat16)[None, None],
        first_new.astype(jnp.bfloat16)[None, None],
        second_new.astype(jnp.bfloat16)[None, None],
    )


def solution(mesh):
    placed = (
        P("pp", "ep", None),
        P("pp", "ep", None),
        P("pp", "ep", None),
        P("pp", "ep", None, None),
        P("pp", "ep", None, None),
        P("pp", "ep", None, None),
        P("pp", "ep", None, None),
    )
    return jax.shard_map(
        shards,
        mesh=mesh,
        in_specs=placed,
        out_specs=(
            P("pp", "ep", None),
            P("pp", "ep", None, None),
            P("pp", "ep", None, None),
            P("pp", "ep", None, None),
        ),
        check_vma=False,
    )
```

time: 493 us -> 247 us (0.50)
  waiting for transfers between devices: 370 us -> 57.6 us
  starting transfers between devices: 54.4 us -> 133 us
  Pallas kernels: 0 us -> 31.1 us
  matrix products: 20.7 us -> 0 us
  local copies, waits for them, and re-layouts: 29.3 us -> 12.9 us
  other arithmetic: 17 us -> 10.1 us
    ppermute x6 -> x21, waiting for transfers between devices: 358 us -> 53.4 us  [the longest x16 45.7 us: send_chips(): lax.ppermute(block, 'ep', [(i, (i + 2 * hops) % count) for i in range(cou...]
    ppermute x6 -> x21, starting transfers between devices: 21.5 us -> 103 us  [the longest x16 77 us: send_chips(): lax.ppermute(block, 'ep', [(i, (i + 2 * hops) % count) for i in range(cou...]
    pallas_call x0 -> x7, Pallas kernels: none -> 31.1 us  [the longest x3 13.7 us: round_call(): pl.pallas_call(kernel, grid_spec=pltpu.PrefetchScalarGridSpec(num_scalar_...]
    dot_general x5 -> x0, matrix products: 20.7 us -> none  [the longest x4 12.3 us: block_dots(): output = jnp.dot(part_hidden, weight, preferred_element_type=jnp.float32)]
    gather x4 -> x0, local copies, waits for them, and re-layouts: 10 us -> none  [the longest x2 7.93 us: shards(): jnp.take(padded, inverse, axis=0)]
    mul x4 -> x0, local copies, waits for them, and re-layouts: 8.99 us -> none  [the longest x3 8.85 us: shards(): gate_dev[:, :, None] * rows_in[:, None, :].astype(jnp.float32)]
    all_to_all x2, waiting for transfers between devices: 11.7 us -> 4.23 us  [the longest x1 4.22 us: shards(): meta = lax.all_to_all(meta, 'ep', split_axis=0, concat_axis=0, tiled=True)]
    select_n x5 -> x0, other arithmetic: 6.2 us -> none  [the longest x2 6.14 us: shards(): jnp.where(level_bit == 0, jnp.concatenate([hidden, partner_rows], axis=0)...]
  transfers between devices with their start and end apart: 8 -> 23, of which waited for: 6 -> 7; matrix products, arithmetic and copies ran while one was open for 5% -> 3% of each run, Pallas kernels for 0% -> 11%
where the time goes in v1:
time: 247 us; the launch traced here: 246 us
  starting transfers between devices  133 us (54%)
  waiting for transfers between devices  57.6 us (23%)
  Pallas kernels  31.1 us (13%)
  local copies, waits for them, and re-layouts  12.9 us (5%)
  other arithmetic  10.1 us (4%)
    ppermute x16, starting transfers between devices, send_chips(): lax.ppermute(block, 'ep', [(i, (i + 2 * hops) % count) for i in range(cou...  77 us
    ppermute x16, waiting for transfers between devices, send_chips(): lax.ppermute(block, 'ep', [(i, (i + 2 * hops) % count) for i in range(cou...  45.7 us
    all_to_all x1, starting transfers between devices, shards(): meta = lax.all_to_all(meta, 'ep', split_axis=0, concat_axis=0, tiled=True)  20.1 us
    ppermute x4, starting transfers between devices, swap_bits(): return lax.ppermute(block, 'ep', [(i, i ^ bits) for i in range(count)])  16.6 us
    pallas_call x3, Pallas kernels, round_call(): pl.pallas_call(kernel, grid_spec=pltpu.PrefetchScalarGridSpec(num_scalar_...  13.7 us
    pallas_call x1, Pallas kernels, place_rows(): pl.pallas_call(place_kernel, grid_spec=pltpu.PrefetchScalarGridSpec(num_s...  12.5 us
    all_to_all x1, starting transfers between devices, shards(): lax.all_to_all(dots, 'ep', split_axis=0, concat_axis=0, tiled=True)  9.76 us
    ppermute x1, starting transfers between devices, shards(): lax.ppermute(moving, 'pp', [(i, rank_count - 1 - i) for i in range(rank_c...  9.31 us
  transfers between devices with their start and end apart: 23, of which 7 were waited for; matrix products, arithmetic and copies ran while one was open for 3% of the time, Pallas kernels for 11%

profile of v1, /device:TPU:1, one launch (start us, length us, event | category | flops | bytes accessed | tf_op | source)
XLA Modules:
  0.0 245.6 jit_solution(2881161084468517478)
XLA Ops:
  2.2 8.8 %collective-permute-start = (bf16[2,128,896]{2,1,0:T(8,128)(2,1)S(1)}, bf16[2,128,896]{2,1,0:T(8,128)(2,1)S(1)}, u32[]{:S(2)}, u32[]{:S(2)}) collective-permute-start(bf16[2,128,896]{2,1,0:T(8,128)(2,1)S(1)} %pad_maximum_fusion.1), channel_id=1, source_target_pairs={{0,1},{1,0},{2,3},{3,2},{4,5},{5,4},{6,7},{7,6},{8,9},{9,8},{10,11... | collective-permute-start | bytes 1376264 | tf_op jit(solution)/shard_map/ppermute | solution.py:33
  17.2 5.0 %collective-permute-start.4 = (bf16[256,896]{1,0:T(8,128)(2,1)}, bf16[256,896]{1,0:T(8,128)(2,1)S(1)}, u32[]{:S(2)}, u32[]{:S(2)}) collective-permute-start(bf16[256,896]{1,0:T(8,128)(2,1)} %pad_maximum_fusion.3), channel_id=1, source_target_pairs={{0,30},{1,31},{2,0},{3,1},{4,2},{5,3},{6,4},{7,5},{8,6},{9,7},{10,... | collective-permute-start | bytes 1376264 | tf_op jit(solution)/shard_map/ppermute | solution.py:28
  26.7 27.6 %collective-permute-done.3.refs_1_ = bf16[256,896]{1,0:T(8,128)(2,1)S(1)} collective-permute-done((bf16[256,896]{1,0:T(8,128)(2,1)}, bf16[256,896]{1,0:T(8,128)(2,1)S(1)}, u32[]{:S(2)}, u32[]{:S(2)}) %collective-permute-start.3) | collective-permute-done | bytes 458784 | tf_op jit(solution)/shard_map/ppermute | solution.py:28
  54.3 6.7 %collective-permute-start.2 = (bf16[256,896]{1,0:T(8,128)(2,1)S(1)}, bf16[256,896]{1,0:T(8,128)(2,1)S(1)}, u32[]{:S(2)}, u32[]{:S(2)}) collective-permute-start(bf16[256,896]{1,0:T(8,128)(2,1)S(1)} %pad_maximum_fusion.2.refs_0_), channel_id=1, source_target_pairs={{0,28},{1,29},{2,30},{3,31},{4,0},{5,1},{6,2},{7,3},{8,4},{9,5},{1... | collective-permute-start | bytes 1376264 | tf_op jit(solution)/shard_map/ppermute | solution.py:28
  71.3 6.2 %collective-permute-start.9 = (bf16[256,896]{1,0:T(8,128)(2,1)S(1)}, bf16[256,896]{1,0:T(8,128)(2,1)}, u32[]{:S(2)}, u32[]{:S(2)}) collective-permute-start(bf16[256,896]{1,0:T(8,128)(2,1)S(1)} %collective-permute-done.4.refs_2_), channel_id=1, source_target_pairs={{0,28},{1,29},{2,30},{3,31},{4,0},{5,1},{6,2},{7,3},{8,4},{9,5},{1... | collective-permute-start | bytes 1376264 | tf_op jit(solution)/shard_map/ppermute | solution.py:28
  81.0 5.5 %collective-permute-start.13 = (bf16[256,896]{1,0:T(8,128)(2,1)S(1)}, bf16[256,896]{1,0:T(8,128)(2,1)}, u32[]{:S(2)}, u32[]{:S(2)}) collective-permute-start(bf16[256,896]{1,0:T(8,128)(2,1)S(1)} %collective-permute-done.2.refs_4_), channel_id=1, source_target_pairs={{0,28},{1,29},{2,30},{3,31},{4,0},{5,1},{6,2},{7,3},{8,4},{9,5},{1... | collective-permute-start | bytes 1376264 | tf_op jit(solution)/shard_map/ppermute | solution.py:28
  88.1 20.1 %all-to-all-start = ((f32[32,8,128]{2,1,0:T(8,128)}), f32[32,8,128]{2,1,0:T(8,128)S(1)}, u32[]{:S(2)}, u32[]{:S(2)}) async-start(f32[32,8,128]{2,1,0:T(8,128)} %broadcast_in_dim.32), calls=%async_computation | async-start | bytes 262144 | tf_op jit(solution)/shard_map/all_to_all | solution.py:262
  108.2 4.2 %collective-permute-start.16 = (bf16[256,896]{1,0:T(8,128)(2,1)}, bf16[256,896]{1,0:T(8,128)(2,1)S(1)}, u32[]{:S(2)}, u32[]{:S(2)}) collective-permute-start(bf16[256,896]{1,0:T(8,128)(2,1)} %collective-permute-done.12.refs_2_), channel_id=1, source_target_pairs={{0,4},{1,5},{2,6},{3,7},{4,8},{5,9},{6,10},{7,11},{8,12},{9,13},{1... | collective-permute-start | bytes 1376264 | tf_op jit(solution)/shard_map/ppermute | solution.py:28
  115.6 3.9 %collective-permute-start.10 = (bf16[256,896]{1,0:T(8,128)(2,1)}, bf16[256,896]{1,0:T(8,128)(2,1)}, u32[]{:S(2)}, u32[]{:S(2)}) collective-permute-start(bf16[256,896]{1,0:T(8,128)(2,1)} %collective-permute-done.8.refs_0_), channel_id=1, source_target_pairs={{0,4},{1,5},{2,6},{3,7},{4,8},{5,9},{6,10},{7,11},{8,12},{9,13},{1... | collective-permute-start | bytes 1376264 | tf_op jit(solution)/shard_map/ppermute | solution.py:28
  119.6 3.5 %collective-permute-start.11 = (bf16[256,896]{1,0:T(8,128)(2,1)}, bf16[256,896]{1,0:T(8,128)(2,1)}, u32[]{:S(2)}, u32[]{:S(2)}) collective-permute-start(bf16[256,896]{1,0:T(8,128)(2,1)} %collective-permute-done.9.refs_1_), channel_id=1, source_target_pairs={{0,28},{1,29},{2,30},{3,31},{4,0},{5,1},{6,2},{7,3},{8,4},{9,5},{1... | collective-permute-start | bytes 1376264 | tf_op jit(solution)/shard_map/ppermute | solution.py:28
  123.0 3.4 %pad_maximum_fusion.rows = bf16[3840,512]{1,0:T(8,128)(2,1)} fusion(bf16[960,512]{1,0:T(8,128)(2,1)} %collective-permute-done.7, bf16[960,512]{1,0:T(8,128)(2,1)} %collective-permute-done.6, bf16[960,512]{1,0:T(8,128)(2,1)} %collective-permute-done.5, bf16[960,512]{1,0:T(8,128)(2,1)S(1)} %bitcast.60), kind=kLoop, calls=%fused_computation | loop fusion | flops 15728640 | bytes 7864320 | tf_op jit(solution)/shard_map/concatenate | solution.py:263
  126.4 4.2 %all-to-all-done.meta = f32[32,8,128]{2,1,0:T(8,128)S(1)} async-done(((f32[32,8,128]{2,1,0:T(8,128)}), f32[32,8,128]{2,1,0:T(8,128)S(1)}, u32[]{:S(2)}, u32[]{:S(2)}) %all-to-all-start) | async-done | bytes 131104 | tf_op jit(solution)/shard_map/all_to_all | solution.py:262
  132.8 12.5 %place_rows.1 = bf16[16,256,512]{2,1,0:T(8,128)(2,1)S(1)} custom-call(s32[66]{0:T(128)S(1)} %concatenate.18.index.ix, f32[32,8,128]{2,1,0:T(8,128)S(1)} %all-to-all-done.meta, bf16[3840,512]{1,0:T(8,128)(2,1)S(1)} %copy-done), custom_call_target="tpu_custom_call" | custom-call | flops 1258291200 | bytes 8388608 | tf_op jit(solution)/shard_map/place_rows/pallas_call | solution.py:64
  147.0 3.9 %round_blocks.3 = (f32[512,896]{1,0:T(8,128)S(1)}, f32[32,1,128]{2,1,0:T(1,128)}) custom-call(s32[66]{0:T(128)S(1)} %concatenate.18.index.ix, bf16[5,256,512]{2,1,0:T(8,128)(2,1)S(1)} %slice.35.hid, bf16[512,896]{1,0:T(8,128)(2,1)S(1)} %bitcast.54, bf16[256,896]{1,0:T(8,128)(2,1)S(1)} %pad_maximum_fusion.2.refs_0_, bf16[256,896]{1,0:T(8,128)(2,1)S(1)} %copy-done.6, ...), custom_call_target="tpu_custom_call" | custom-call | flops 2348810240 | bytes 7274496 | tf_op jit(solution)/shard_map/round_blocks/pallas_call | solution.py:131
  151.1 8.6 %collective-permute-start.18 = (bf16[128,896]{1,0:T(8,128)(2,1)S(1)}, bf16[128,896]{1,0:T(8,128)(2,1)S(1)}, u32[]{:S(2)}, u32[]{:S(2)}) collective-permute-start(bf16[128,896]{1,0:T(8,128)(2,1)S(1)} %slice.28), channel_id=1, source_target_pairs={{0,4},{1,5},{2,6},{3,7},{4,8},{5,9},{6,10},{7,11},{8,12},{9,13},{1... | collective-permute-start | bytes 688136 | tf_op jit(solution)/shard_map/ppermute | solution.py:28
  163.5 16.3 %collective-permute-start.14 = (bf16[256,896]{1,0:T(8,128)(2,1)}, bf16[256,896]{1,0:T(8,128)(2,1)S(1)}, u32[]{:S(2)}, u32[]{:S(2)}) collective-permute-start(bf16[256,896]{1,0:T(8,128)(2,1)} %collective-permute-done.10.refs_0_), channel_id=1, source_target_pairs={{0,4},{1,5},{2,6},{3,7},{4,8},{5,9},{6,10},{7,11},{8,12},{9,13},{1... | collective-permute-start | bytes 1376264 | tf_op jit(solution)/shard_map/ppermute | solution.py:28
  181.8 4.9 %round_blocks.4 = (f32[512,896]{1,0:T(8,128)S(1)}, f32[32,1,128]{2,1,0:T(1,128)}) custom-call(s32[66]{0:T(128)S(1)} %concatenate.18.index.ix, bf16[4,256,512]{2,1,0:T(8,128)(2,1)S(1)} %get-tuple-element.44.hid, bf16[512,896]{1,0:T(8,128)(2,1)S(1)} %bitcast.55, ...), custom_call_target="tpu_custom_call", output_to_operand_aliasing={{0}: (7, {}), {1}: (8, {})} | custom-call | flops 1879048192 | bytes 6553600 | tf_op jit(solution)/shard_map/round_blocks/pallas_call | solution.py:131
  186.7 4.8 %round_blocks.5 = (f32[512,896]{1,0:T(8,128)S(1)}, f32[32,1,128]{2,1,0:T(1,128)}) custom-call(s32[66]{0:T(128)S(1)} %concatenate.18.index.ix, bf16[4,256,512]{2,1,0:T(8,128)(2,1)S(1)} %get-tuple-element.45.hid, bf16[512,896]{1,0:T(8,128)(2,1)S(1)} %bitcast.56, ...), custom_call_target="tpu_custom_call", output_to_operand_aliasing={{0}: (7, {}), {1}: (8, {})} | custom-call | flops 1879048192 | bytes 6553600 | tf_op jit(solution)/shard_map/round_blocks/pallas_call | solution.py:131
  191.6 6.0 %collective-permute-done.14.refs_0_ = bf16[256,896]{1,0:T(8,128)(2,1)S(1)} collective-permute-done((bf16[256,896]{1,0:T(8,128)(2,1)}, bf16[256,896]{1,0:T(8,128)(2,1)S(1)}, u32[]{:S(2)}, u32[]{:S(2)}) %collective-permute-start.14) | collective-permute-done | bytes 458784 | tf_op jit(solution)/shard_map/ppermute | solution.py:28
  197.7 7.9 %collective-permute-done.15.refs_1_ = bf16[256,896]{1,0:T(8,128)(2,1)S(1)} collective-permute-done((bf16[256,896]{1,0:T(8,128)(2,1)}, bf16[256,896]{1,0:T(8,128)(2,1)S(1)}, u32[]{:S(2)}, u32[]{:S(2)}) %collective-permute-start.15) | collective-permute-done | bytes 458784 | tf_op jit(solution)/shard_map/ppermute | solution.py:28
  209.3 9.8 %all-to-all-start.1 = ((f32[32,1,128]{2,1,0:T(1,128)}), f32[32,1,128]{2,1,0:T(1,128)S(1)}, u32[]{:S(2)}, u32[]{:S(2)}) async-start(f32[32,1,128]{2,1,0:T(1,128)} %last_dots.1), calls=%async_computation.1 | async-start | bytes 32768 | tf_op jit(solution)/shard_map/all_to_all | solution.py:294
  221.5 9.3 %collective-permute-start.20 = (bf16[256,896]{1,0:T(8,128)(2,1)}, bf16[256,896]{1,0:T(8,128)(2,1)}, u32[]{:S(2)}, u32[]{:S(2)}) collective-permute-start(bf16[256,896]{1,0:T(8,128)(2,1)} %last_grads.3), channel_id=1, source_target_pairs={{0,480},{32,448},{64,416},{96,384},{128,352},{160,320},{192,288},{... | collective-permute-start | bytes 1376264 | tf_op jit(solution)/shard_map/ppermute | solution.py:292
  234.1 7.7 %collective-permute-done.20 = bf16[256,896]{1,0:T(8,128)(2,1)} collective-permute-done((bf16[256,896]{1,0:T(8,128)(2,1)}, bf16[256,896]{1,0:T(8,128)(2,1)}, u32[]{:S(2)}, u32[]{:S(2)}) %collective-permute-start.20) | collective-permute-done | bytes 458784 | tf_op jit(solution)/shard_map/ppermute | solution.py:292
  241.8 3.8 %convert_bitcast_fusion = (bf16[1,1,256,896]{3,2,1,0:T(8,128)(2,1)}, bf16[1,1,256,896]{3,2,1,0:T(8,128)(2,1)}, bf16[1,1,256,896]{3,2,1,0:T(8,128)(2,1)}) fusion(bf16[256,896]{1,0:T(8,128)(2,1)} %collective-permute-done.20, bf16[256,896]{1,0:T(8,128)(2,1)} %copy-done.4, bf16[1,1,256,896]{3,2,1,0:T(8,128)(2,1)} %param.14, bf16[1,1,256,896]{3,2,1,0:T(8,128)(2,1)} %param.13, ...), kind=kLoop, calls=%fused_computation.15 | loop fusion | flops 5505024 | bytes 3670020 | tf_op jit(solution)/shard_map/broadcast_in_dim | solution.py:319
  (90 shorter events, 49.7 us)
Async XLA Ops:
  0.7 86.6 %copy-start.15 = (s32[1,128,2]{1,2,0:T(2,128)S(1)}, s32[1,128,2]{1,2,0:T(2,128)}, u32[]{:S(2)}) copy-start(s32[1,128,2]{1,2,0:T(2,128)} %param.9) | copy-start | bytes 3076
  2.2 10.7 %collective-permute-start = (bf16[2,128,896]{2,1,0:T(8,128)(2,1)S(1)}, bf16[2,128,896]{2,1,0:T(8,128)(2,1)S(1)}, u32[]{:S(2)}, u32[]{:S(2)}) collective-permute-start(bf16[2,128,896]{2,1,0:T(8,128)(2,1)S(1)} %pad_maximum_fusion.1), channel_id=1, source_target_pairs={{0,1},{1,0},{2,3},{3,2},{4,5},{5,4},{6,7},{7,6},{8,9},{9,8},{10,11... | collective-permute-start | bytes 1376264 | tf_op jit(solution)/shard_map/ppermute | solution.py:33
  11.0 52.7 %collective-permute-start.6 = (bf16[960,512]{1,0:T(8,128)(2,1)}, bf16[960,512]{1,0:T(8,128)(2,1)}, u32[]{:S(2)}, u32[]{:S(2)}) collective-permute-start(bf16[960,512]{1,0:T(8,128)(2,1)} %bitcast.58), channel_id=1, source_target_pairs={{0,2},{1,3},{2,0},{3,1},{4,6},{5,7},{6,4},{7,5},{8,10},{9,11},{10,... | collective-permute-start | bytes 2949128 | tf_op jit(solution)/shard_map/ppermute | solution.py:33
  13.8 40.5 %collective-permute-start.3 = (bf16[256,896]{1,0:T(8,128)(2,1)}, bf16[256,896]{1,0:T(8,128)(2,1)S(1)}, u32[]{:S(2)}, u32[]{:S(2)}) collective-permute-start(bf16[256,896]{1,0:T(8,128)(2,1)} %pad_maximum_fusion.3), channel_id=1, source_target_pairs={{0,2},{1,3},{2,4},{3,5},{4,6},{5,7},{6,8},{7,9},{8,10},{9,11},{10,... | collective-permute-start | bytes 1376264 | tf_op jit(solution)/shard_map/ppermute | solution.py:28
  17.2 43.8 %collective-permute-start.4 = (bf16[256,896]{1,0:T(8,128)(2,1)}, bf16[256,896]{1,0:T(8,128)(2,1)S(1)}, u32[]{:S(2)}, u32[]{:S(2)}) collective-permute-start(bf16[256,896]{1,0:T(8,128)(2,1)} %pad_maximum_fusion.3), channel_id=1, source_target_pairs={{0,30},{1,31},{2,0},{3,1},{4,2},{5,3},{6,4},{7,5},{8,6},{9,7},{10,... | collective-permute-start | bytes 1376264 | tf_op jit(solution)/shard_map/ppermute | solution.py:28
  22.2 97.4 %collective-permute-start.5 = (bf16[960,512]{1,0:T(8,128)(2,1)S(1)}, bf16[960,512]{1,0:T(8,128)(2,1)}, u32[]{:S(2)}, u32[]{:S(2)}) collective-permute-start(bf16[960,512]{1,0:T(8,128)(2,1)S(1)} %bitcast.59), channel_id=1, source_target_pairs={{0,1},{1,0},{2,3},{3,2},{4,5},{5,4},{6,7},{7,6},{8,9},{9,8},{10,11... | collective-permute-start | bytes 2949128 | tf_op jit(solution)/shard_map/ppermute | solution.py:33
  24.7 44.9 %collective-permute-start.1 = (bf16[256,896]{1,0:T(8,128)(2,1)S(1)}, bf16[256,896]{1,0:T(8,128)(2,1)S(1)}, u32[]{:S(2)}, u32[]{:S(2)}) collective-permute-start(bf16[256,896]{1,0:T(8,128)(2,1)S(1)} %pad_maximum_fusion.2.refs_0_), channel_id=1, source_target_pairs={{0,4},{1,5},{2,6},{3,7},{4,8},{5,9},{6,10},{7,11},{8,12},{9,13},{1... | collective-permute-start | bytes 1376264 | tf_op jit(solution)/shard_map/ppermute | solution.py:28
  54.3 17.1 %collective-permute-start.2 = (bf16[256,896]{1,0:T(8,128)(2,1)S(1)}, bf16[256,896]{1,0:T(8,128)(2,1)S(1)}, u32[]{:S(2)}, u32[]{:S(2)}) collective-permute-start(bf16[256,896]{1,0:T(8,128)(2,1)S(1)} %pad_maximum_fusion.2.refs_0_), channel_id=1, source_target_pairs={{0,28},{1,29},{2,30},{3,31},{4,0},{5,1},{6,2},{7,3},{8,4},{9,5},{1... | collective-permute-start | bytes 1376264 | tf_op jit(solution)/shard_map/ppermute | solution.py:28
  61.0 20.1 %collective-permute-start.8 = (bf16[256,896]{1,0:T(8,128)(2,1)S(1)}, bf16[256,896]{1,0:T(8,128)(2,1)}, u32[]{:S(2)}, u32[]{:S(2)}) collective-permute-start(bf16[256,896]{1,0:T(8,128)(2,1)S(1)} %collective-permute-done.3.refs_1_), channel_id=1, source_target_pairs={{0,4},{1,5},{2,6},{3,7},{4,8},{5,9},{6,10},{7,11},{8,12},{9,13},{1... | collective-permute-start | bytes 1376264 | tf_op jit(solution)/shard_map/ppermute | solution.py:28
  63.7 59.3 %collective-permute-start.7 = (bf16[960,512]{1,0:T(8,128)(2,1)}, bf16[960,512]{1,0:T(8,128)(2,1)}, u32[]{:S(2)}, u32[]{:S(2)}) collective-permute-start(bf16[960,512]{1,0:T(8,128)(2,1)} %collective-permute-done.6), channel_id=1, source_target_pairs={{0,1},{1,0},{2,3},{3,2},{4,5},{5,4},{6,7},{7,6},{8,9},{9,8},{10,11... | collective-permute-start | bytes 2949128 | tf_op jit(solution)/shard_map/ppermute | solution.py:33
  71.3 36.8 %collective-permute-start.9 = (bf16[256,896]{1,0:T(8,128)(2,1)S(1)}, bf16[256,896]{1,0:T(8,128)(2,1)}, u32[]{:S(2)}, u32[]{:S(2)}) collective-permute-start(bf16[256,896]{1,0:T(8,128)(2,1)S(1)} %collective-permute-done.4.refs_2_), channel_id=1, source_target_pairs={{0,28},{1,29},{2,30},{3,31},{4,0},{5,1},{6,2},{7,3},{8,4},{9,5},{1... | collective-permute-start | bytes 1376264 | tf_op jit(solution)/shard_map/ppermute | solution.py:28
  78.3 29.8 %collective-permute-start.12 = (bf16[256,896]{1,0:T(8,128)(2,1)S(1)}, bf16[256,896]{1,0:T(8,128)(2,1)}, u32[]{:S(2)}, u32[]{:S(2)}) collective-permute-start(bf16[256,896]{1,0:T(8,128)(2,1)S(1)} %collective-permute-done.1.refs_3_), channel_id=1, source_target_pairs={{0,4},{1,5},{2,6},{3,7},{4,8},{5,9},{6,10},{7,11},{8,12},{9,13},{1... | collective-permute-start | bytes 1376264 | tf_op jit(solution)/shard_map/ppermute | solution.py:28
  81.0 27.2 %collective-permute-start.13 = (bf16[256,896]{1,0:T(8,128)(2,1)S(1)}, bf16[256,896]{1,0:T(8,128)(2,1)}, u32[]{:S(2)}, u32[]{:S(2)}) collective-permute-start(bf16[256,896]{1,0:T(8,128)(2,1)S(1)} %collective-permute-done.2.refs_4_), channel_id=1, source_target_pairs={{0,28},{1,29},{2,30},{3,31},{4,0},{5,1},{6,2},{7,3},{8,4},{9,5},{1... | collective-permute-start | bytes 1376264 | tf_op jit(solution)/shard_map/ppermute | solution.py:28
  88.1 42.6 %all-to-all-start = ((f32[32,8,128]{2,1,0:T(8,128)}), f32[32,8,128]{2,1,0:T(8,128)S(1)}, u32[]{:S(2)}, u32[]{:S(2)}) async-start(f32[32,8,128]{2,1,0:T(8,128)} %broadcast_in_dim.32), calls=%async_computation | async-start | bytes 262144 | tf_op jit(solution)/shard_map/all_to_all | solution.py:262
  108.2 42.8 %collective-permute-start.16 = (bf16[256,896]{1,0:T(8,128)(2,1)}, bf16[256,896]{1,0:T(8,128)(2,1)S(1)}, u32[]{:S(2)}, u32[]{:S(2)}) collective-permute-start(bf16[256,896]{1,0:T(8,128)(2,1)} %collective-permute-done.12.refs_2_), channel_id=1, source_target_pairs={{0,4},{1,5},{2,6},{3,7},{4,8},{5,9},{6,10},{7,11},{8,12},{9,13},{1... | collective-permute-start | bytes 1376264 | tf_op jit(solution)/shard_map/ppermute | solution.py:28
  112.4 38.6 %collective-permute-start.17 = (bf16[256,896]{1,0:T(8,128)(2,1)}, bf16[256,896]{1,0:T(8,128)(2,1)}, u32[]{:S(2)}, u32[]{:S(2)}) collective-permute-start(bf16[256,896]{1,0:T(8,128)(2,1)} %collective-permute-done.13.refs_3_), channel_id=1, source_target_pairs={{0,28},{1,29},{2,30},{3,31},{4,0},{5,1},{6,2},{7,3},{8,4},{9,5},{1... | collective-permute-start | bytes 1376264 | tf_op jit(solution)/shard_map/ppermute | solution.py:28
  115.6 35.4 %collective-permute-start.10 = (bf16[256,896]{1,0:T(8,128)(2,1)}, bf16[256,896]{1,0:T(8,128)(2,1)}, u32[]{:S(2)}, u32[]{:S(2)}) collective-permute-start(bf16[256,896]{1,0:T(8,128)(2,1)} %collective-permute-done.8.refs_0_), channel_id=1, source_target_pairs={{0,4},{1,5},{2,6},{3,7},{4,8},{5,9},{6,10},{7,11},{8,12},{9,13},{1... | collective-permute-start | bytes 1376264 | tf_op jit(solution)/shard_map/ppermute | solution.py:28
  119.6 31.5 %collective-permute-start.11 = (bf16[256,896]{1,0:T(8,128)(2,1)}, bf16[256,896]{1,0:T(8,128)(2,1)}, u32[]{:S(2)}, u32[]{:S(2)}) collective-permute-start(bf16[256,896]{1,0:T(8,128)(2,1)} %collective-permute-done.9.refs_1_), channel_id=1, source_target_pairs={{0,28},{1,29},{2,30},{3,31},{4,0},{5,1},{6,2},{7,3},{8,4},{9,5},{1... | collective-permute-start | bytes 1376264 | tf_op jit(solution)/shard_map/ppermute | solution.py:28
  151.1 40.4 %collective-permute-start.18 = (bf16[128,896]{1,0:T(8,128)(2,1)S(1)}, bf16[128,896]{1,0:T(8,128)(2,1)S(1)}, u32[]{:S(2)}, u32[]{:S(2)}) collective-permute-start(bf16[128,896]{1,0:T(8,128)(2,1)S(1)} %slice.28), channel_id=1, source_target_pairs={{0,4},{1,5},{2,6},{3,7},{4,8},{5,9},{6,10},{7,11},{8,12},{9,13},{1... | collective-permute-start | bytes 688136 | tf_op jit(solution)/shard_map/ppermute | solution.py:28
  160.6 30.9 %collective-permute-start.19 = (bf16[128,896]{1,0:T(8,128)(2,1)S(1)}, bf16[128,896]{1,0:T(8,128)(2,1)S(1)}, u32[]{:S(2)}, u32[]{:S(2)}) collective-permute-start(bf16[128,896]{1,0:T(8,128)(2,1)S(1)} %slice.29), channel_id=1, source_target_pairs={{0,28},{1,29},{2,30},{3,31},{4,0},{5,1},{6,2},{7,3},{8,4},{9,5},{1... | collective-permute-start | bytes 688136 | tf_op jit(solution)/shard_map/ppermute | solution.py:28
  163.5 34.1 %collective-permute-start.14 = (bf16[256,896]{1,0:T(8,128)(2,1)}, bf16[256,896]{1,0:T(8,128)(2,1)S(1)}, u32[]{:S(2)}, u32[]{:S(2)}) collective-permute-start(bf16[256,896]{1,0:T(8,128)(2,1)} %collective-permute-done.10.refs_0_), channel_id=1, source_target_pairs={{0,4},{1,5},{2,6},{3,7},{4,8},{5,9},{6,10},{7,11},{8,12},{9,13},{1... | collective-permute-start | bytes 1376264 | tf_op jit(solution)/shard_map/ppermute | solution.py:28
  179.9 25.7 %collective-permute-start.15 = (bf16[256,896]{1,0:T(8,128)(2,1)}, bf16[256,896]{1,0:T(8,128)(2,1)S(1)}, u32[]{:S(2)}, u32[]{:S(2)}) collective-permute-start(bf16[256,896]{1,0:T(8,128)(2,1)} %collective-permute-done.11.refs_1_), channel_id=1, source_target_pairs={{0,28},{1,29},{2,30},{3,31},{4,0},{5,1},{6,2},{7,3},{8,4},{9,5},{1... | collective-permute-start | bytes 1376264 | tf_op jit(solution)/shard_map/ppermute | solution.py:28
  209.3 22.9 %all-to-all-start.1 = ((f32[32,1,128]{2,1,0:T(1,128)}), f32[32,1,128]{2,1,0:T(1,128)S(1)}, u32[]{:S(2)}, u32[]{:S(2)}) async-start(f32[32,1,128]{2,1,0:T(1,128)} %last_dots.1), calls=%async_computation.1 | async-start | bytes 32768 | tf_op jit(solution)/shard_map/all_to_all | solution.py:294
  221.5 20.4 %collective-permute-start.20 = (bf16[256,896]{1,0:T(8,128)(2,1)}, bf16[256,896]{1,0:T(8,128)(2,1)}, u32[]{:S(2)}, u32[]{:S(2)}) collective-permute-start(bf16[256,896]{1,0:T(8,128)(2,1)} %last_grads.3), channel_id=1, source_target_pairs={{0,480},{32,448},{64,416},{96,384},{128,352},{160,320},{192,288},{... | collective-permute-start | bytes 1376264 | tf_op jit(solution)/shard_map/ppermute | solution.py:292
  (16 other events, 189.5 us)

commit v2 on v1

--- a/solution.py
+++ b/solution.py
@@ -58,23 +58,24 @@
         out[0, half * tokens : (half + 1) * tokens, :] = (gate * picked).astype(out.dtype)
 
 
-def place_rows(index, meta, hidden):
+def place_rows(index, meta, hidden, start, stop):
     tokens = meta.shape[2]
     units = hidden.shape[1]
+    count = stop - start
     return pl.pallas_call(
         place_kernel,
         grid_spec=pltpu.PrefetchScalarGridSpec(
             num_scalar_prefetch=1,
-            grid=(16,),
+            grid=(count,),
             in_specs=[
-                pl.BlockSpec((2, 8, tokens), lambda i, ix: (ix[i], 0, 0)),
-                pl.BlockSpec((2 * CAP, units), lambda i, ix: (ix[18 + i], 0)),
+                pl.BlockSpec((2, 8, tokens), lambda i, ix: (ix[start + i], 0, 0)),
+                pl.BlockSpec((2 * CAP, units), lambda i, ix: (ix[18 + start + i], 0)),
             ],
             out_specs=pl.BlockSpec((1, 2 * tokens, units), lambda i, ix: (i, 0, 0)),
         ),
-        out_shape=jax.ShapeDtypeStruct((16, 2 * tokens, units), jnp.bfloat16),
+        out_shape=jax.ShapeDtypeStruct((count, 2 * tokens, units), jnp.bfloat16),
         cost_estimate=pl.CostEstimate(
-            flops=2 * 16 * 256 * 240 * (units + 128), bytes_accessed=16 * 512 * units * 2, transcendentals=0
+            flops=2 * count * 256 * 240 * (units + 128), bytes_accessed=count * 512 * units * 2, transcendentals=0
         ),
         compiler_params=pltpu.CompilerParams(vmem_limit_bytes=VMEM_BYTES),
         name="place_rows",
@@ -233,56 +234,46 @@
     def features(at):
         return lax.dynamic_slice(rows_in, (0, at * part), (tokens, part))
 
+    tie = lax.optimization_barrier
+    own_hidden = hidden_saved[0, 0]
+    chip_hidden = swap_bits(own_hidden, 2)
     outgoing = jnp.stack([features(block ^ 1), features(block ^ 3)])
     incoming = swap_bits(outgoing, 1)
+    core_hidden = swap_bits(own_hidden, 1)
     same = jnp.concatenate([features(block), incoming[0]], axis=0)
     diff = jnp.concatenate([features(block ^ 2), incoming[1]], axis=0)
-
-    own_hidden = hidden_saved[0, 0]
-    chip_hidden = swap_bits(own_hidden, 2)
     meta = jnp.concatenate([route_dev.astype(jnp.float32), gate_dev], axis=1)
     meta = jnp.pad(meta.T, ((0, 4), (0, 0)))
     meta = jnp.broadcast_to(meta[None], (lax.axis_size("ep"),) + meta.shape)
-
-    diff_steps = [(send_chips(diff, 1), send_chips(diff, -1))]
-    same_steps = [(send_chips(same, 2), send_chips(same, -2))]
-    grads = dots = placed = None
-    for step in range(1, 4):
-        ahead = diff_steps[-1] if step == 1 else diff_steps[-1] + same_steps[-2]
-        if step == 3:
-            ahead = ahead + (placed,)
-        ahead = lax.optimization_barrier(ahead)
-        diff_steps.append((send_chips(ahead[0], 2), send_chips(ahead[1], -2)))
-        ahead = same_steps[-1] + diff_steps[-2]
-        if step == 3:
-            ahead = ahead + (grads,)
-        ahead = lax.optimization_barrier(ahead)
-        if step == 1:
-            meta = lax.optimization_barrier((meta,) + ahead[:2])[0]
-            meta = lax.all_to_all(meta, "ep", split_axis=0, concat_axis=0, tiled=True)
-            hidden = jnp.concatenate(
-                [own_hidden, swap_bits(own_hidden, 1), chip_hidden, swap_bits(chip_hidden, 1)],
-                axis=0,
-            )
-            placed = place_rows(index, meta, hidden)
-        if step < 3:
-            same_steps.append((send_chips(ahead[0], 2), send_chips(ahead[1], -2)))
-        else:
-            across = jnp.concatenate(
-                [send_chips(ahead[0][:tokens], 2), send_chips(ahead[1][tokens:], -2)], axis=0
-            )
-        if step > 1:
-            start, stop = ROUNDS[step - 2]
-            rows = list(diff_steps[step - 2] + same_steps[step - 2])
-            rows = [same] + rows if step == 2 else rows
-            grads, dots = round_call(index, start, rows, placed[start:stop], weight, grads, dots)
-    start, stop = ROUNDS[2]
-    rows = list(diff_steps[2] + same_steps[2])
-    grads, dots = round_call(index, start, rows, placed[start:stop], weight, grads, dots)
-    far_forth, far_back = diff_steps[3]
-    last = [far_forth, far_back, across]
+    meta = lax.all_to_all(meta, "ep", split_axis=0, concat_axis=0, tiled=True)
+    same, diff, chip_hidden, core_hidden = tie((same, diff, chip_hidden, core_hidden))
+
+    def step(pair, hops, *done):
+        pair = tie((*pair, *done)) if done else pair
+        return send_chips(pair[0], hops), send_chips(pair[1], -hops)
+
+    def round_at(number, rows, grads, dots):
+        start, stop = ROUNDS[number]
+        placed = place_rows(index, meta, hidden, start, stop)
+        return round_call(index, start, rows, placed, weight, grads, dots)
+
+    d1 = step((diff, diff), 1)
+    s1 = step((same, same), 2)
+    far_hidden = swap_bits(chip_hidden, 1)
+    hidden = jnp.concatenate([own_hidden, core_hidden, chip_hidden, far_hidden], axis=0)
+    d2 = step(d1, 2)
+    s2 = step(s1, 2, meta)
+    d3 = step(d2, 2)
+    s3 = step(s2, 2)
+    grads, dots = round_at(0, [same, *d1, *s1], None, None)
+    d4 = step(d3, 2)
+    grads1, dots = round_at(1, [*d2, *s2], grads, dots)
+    ahead = tie((*s3,))
+    across = (send_chips(ahead[0][:tokens], 2), send_chips(ahead[1][tokens:], -2))
+    grads, dots = round_at(2, [*d3, *s3], grads1, dots)
     start, stop = ROUNDS[3]
-    placed_last = placed[start:stop]
+    last = [*d4, jnp.concatenate(across, axis=0)]
+    placed_last = place_rows(index, meta, hidden, start, stop)
 
     pipe_rank = lax.axis_index("pp")
     rank_count = lax.axis_size("pp")

time: 247 us -> 223 us (0.903)
  starting transfers between devices: 133 us -> 117 us
  local copies, waits for them, and re-layouts: 12.9 us -> 4.92 us
    all_to_all x1, starting transfers between devices: 20.1 us -> 11.4 us  [shards(): meta = lax.all_to_all(meta, 'ep', split_axis=0, concat_axis=0, tiled=True)]
    ppermute x16, starting transfers between devices: 77 us -> 69.6 us  [send_chips(): lax.ppermute(block, 'ep', [(i, (i + 2 * hops) % count) for i in range(cou...]
    unnamed x35 -> x23, local copies, waits for them, and re-layouts: 9.24 us -> 2.61 us
    all_to_all x1, waiting for transfers between devices: 4.22 us -> 0.01 us  [shards(): meta = lax.all_to_all(meta, 'ep', split_axis=0, concat_axis=0, tiled=True)]
    ppermute x16, waiting for transfers between devices: 45.7 us -> 49.1 us  [send_chips(): lax.ppermute(block, 'ep', [(i, (i + 2 * hops) % count) for i in range(cou...]
    ppermute x1, starting transfers between devices: 9.31 us -> 6.81 us  [shards(): lax.ppermute(moving, 'pp', [(i, rank_count - 1 - i) for i in range(rank_c...]
    pallas_call x1 -> x4, Pallas kernels: 12.5 us -> 14.2 us  [place_rows(): pl.pallas_call(place_kernel, grid_spec=pltpu.PrefetchScalarGridSpec(num_s...]
  transfers between devices with their start and end apart: 23 -> 23, of which waited for: 7 -> 7; matrix products, arithmetic and copies ran while one was open for 3% -> 4% of each run, Pallas kernels for 11% -> 13%
where the time goes in v2:
time: 223 us; the launch traced here: 221 us
  starting transfers between devices  117 us (52%)
  waiting for transfers between devices  56.6 us (25%)
  Pallas kernels  32.3 us (14%)
  other arithmetic  9.57 us (4%)
  local copies, waits for them, and re-layouts  4.92 us (2%)
    ppermute x16, starting transfers between devices, send_chips(): lax.ppermute(block, 'ep', [(i, (i + 2 * hops) % count) for i in range(cou...  69.6 us
    ppermute x16, waiting for transfers between devices, send_chips(): lax.ppermute(block, 'ep', [(i, (i + 2 * hops) % count) for i in range(cou...  49.1 us
    ppermute x4, starting transfers between devices, swap_bits(): return lax.ppermute(block, 'ep', [(i, i ^ bits) for i in range(count)])  17.8 us
    pallas_call x4, Pallas kernels, place_rows(): pl.pallas_call(place_kernel, grid_spec=pltpu.PrefetchScalarGridSpec(num_s...  14.2 us
    pallas_call x3, Pallas kernels, round_call(): pl.pallas_call(kernel, grid_spec=pltpu.PrefetchScalarGridSpec(num_scalar_...  13.1 us
    all_to_all x1, starting transfers between devices, shards(): meta = lax.all_to_all(meta, 'ep', split_axis=0, concat_axis=0, tiled=True)  11.4 us
    all_to_all x1, starting transfers between devices, shards(): lax.all_to_all(dots, 'ep', split_axis=0, concat_axis=0, tiled=True)  11.1 us
    ppermute x1, starting transfers between devices, shards(): lax.ppermute(moving, 'pp', [(i, rank_count - 1 - i) for i in range(rank_c...  6.81 us
  transfers between devices with their start and end apart: 23, of which 7 were waited for; matrix products, arithmetic and copies ran while one was open for 4% of the time, Pallas kernels for 13%

profile of v2, /device:TPU:1, one launch (start us, length us, event | category | flops | bytes accessed | tf_op | source)
XLA Modules:
  0.0 221.4 jit_solution(9975127619688289751)
XLA Ops:
  0.6 4.4 %collective-permute-start.1 = (bf16[960,512]{1,0:T(8,128)(2,1)}, bf16[960,512]{1,0:T(8,128)(2,1)}, u32[]{:S(2)}, u32[]{:S(2)}) collective-permute-start(bf16[960,512]{1,0:T(8,128)(2,1)} %bitcast.58), channel_id=1, source_target_pairs={{0,2},{1,3},{2,0},{3,1},{4,6},{5,7},{6,4},{7,5},{8,10},{9,11},{10,... | collective-permute-start | bytes 2949128 | tf_op jit(solution)/shard_map/ppermute | solution.py:33
  5.0 6.3 %collective-permute-start.2 = (bf16[960,512]{1,0:T(8,128)(2,1)}, bf16[960,512]{1,0:T(8,128)(2,1)}, u32[]{:S(2)}, u32[]{:S(2)}) collective-permute-start(bf16[960,512]{1,0:T(8,128)(2,1)} %bitcast.59), channel_id=1, source_target_pairs={{0,1},{1,0},{2,3},{3,2},{4,5},{5,4},{6,7},{7,6},{8,9},{9,8},{10,11... | collective-permute-start | bytes 2949128 | tf_op jit(solution)/shard_map/ppermute | solution.py:33
  16.8 11.4 %all-to-all-start = ((f32[32,8,128]{2,1,0:T(8,128)}), f32[32,8,128]{2,1,0:T(8,128)S(1)}, u32[]{:S(2)}, u32[]{:S(2)}) async-start(f32[32,8,128]{2,1,0:T(8,128)} %broadcast_in_dim.32), calls=%async_computation | async-start | bytes 262144 | tf_op jit(solution)/shard_map/all_to_all | solution.py:248
  28.4 4.2 %collective-permute-start.12 = (bf16[256,896]{1,0:T(8,128)(2,1)S(1)}, bf16[256,896]{1,0:T(8,128)(2,1)S(1)}, u32[]{:S(2)}, u32[]{:S(2)}) collective-permute-start(bf16[256,896]{1,0:T(8,128)(2,1)S(1)} %get-tuple-element.21.refs_0_), channel_id=1, source_target_pairs={{0,4},{1,5},{2,6},{3,7},{4,8},{5,9},{6,10},{7,11},{8,12},{9,13},{1... | collective-permute-start | bytes 1376264 | tf_op jit(solution)/shard_map/ppermute | solution.py:28
  32.6 11.2 %collective-permute-start.13 = (bf16[256,896]{1,0:T(8,128)(2,1)S(1)}, bf16[256,896]{1,0:T(8,128)(2,1)S(1)}, u32[]{:S(2)}, u32[]{:S(2)}) collective-permute-start(bf16[256,896]{1,0:T(8,128)(2,1)S(1)} %get-tuple-element.21.refs_0_), channel_id=1, source_target_pairs={{0,28},{1,29},{2,30},{3,31},{4,0},{5,1},{6,2},{7,3},{8,4},{9,5},{1... | collective-permute-start | bytes 1376264 | tf_op jit(solution)/shard_map/ppermute | solution.py:28
  45.7 4.6 %collective-permute-start.8 = (bf16[256,896]{1,0:T(8,128)(2,1)S(1)}, bf16[256,896]{1,0:T(8,128)(2,1)S(1)}, u32[]{:S(2)}, u32[]{:S(2)}) collective-permute-start(bf16[256,896]{1,0:T(8,128)(2,1)S(1)} %get-tuple-element.20), channel_id=1, source_target_pairs={{0,30},{1,31},{2,0},{3,1},{4,2},{5,3},{6,4},{7,5},{8,6},{9,7},{10,... | collective-permute-start | bytes 1376264 | tf_op jit(solution)/shard_map/ppermute | solution.py:28
  50.2 5.2 %collective-permute-start.3 = (bf16[960,512]{1,0:T(8,128)(2,1)}, bf16[960,512]{1,0:T(8,128)(2,1)}, u32[]{:S(2)}, u32[]{:S(2)}) collective-permute-start(bf16[960,512]{1,0:T(8,128)(2,1)} %collective-permute-done.1), channel_id=1, source_target_pairs={{0,1},{1,0},{2,3},{3,2},{4,5},{5,4},{6,7},{7,6},{8,9},{9,8},{10,11... | collective-permute-start | bytes 2949128 | tf_op jit(solution)/shard_map/ppermute | solution.py:33
  55.5 5.8 %collective-permute-done.12.refs_3_ = bf16[256,896]{1,0:T(8,128)(2,1)S(1)} collective-permute-done((bf16[256,896]{1,0:T(8,128)(2,1)S(1)}, bf16[256,896]{1,0:T(8,128)(2,1)S(1)}, u32[]{:S(2)}, u32[]{:S(2)}) %collective-permute-start.12) | collective-permute-done | bytes 458784 | tf_op jit(solution)/shard_map/ppermute | solution.py:28
  63.2 6.1 %collective-permute-start.16 = (bf16[256,896]{1,0:T(8,128)(2,1)S(1)}, bf16[256,896]{1,0:T(8,128)(2,1)}, u32[]{:S(2)}, u32[]{:S(2)}) collective-permute-start(bf16[256,896]{1,0:T(8,128)(2,1)S(1)} %collective-permute-done.13.refs_4_), channel_id=1, source_target_pairs={{0,28},{1,29},{2,30},{3,31},{4,0},{5,1},{6,2},{7,3},{8,4},{9,5},{1... | collective-permute-start | bytes 1376264 | tf_op jit(solution)/shard_map/ppermute | solution.py:28
  74.4 4.1 %collective-permute-start.9 = (bf16[256,896]{1,0:T(8,128)(2,1)S(1)}, bf16[256,896]{1,0:T(8,128)(2,1)}, u32[]{:S(2)}, u32[]{:S(2)}) collective-permute-start(bf16[256,896]{1,0:T(8,128)(2,1)S(1)} %collective-permute-done.8.refs_2_), channel_id=1, source_target_pairs={{0,28},{1,29},{2,30},{3,31},{4,0},{5,1},{6,2},{7,3},{8,4},{9,5},{1... | collective-permute-start | bytes 1376264 | tf_op jit(solution)/shard_map/ppermute | solution.py:28
  78.8 16.6 %collective-permute-done.14.refs_2_ = bf16[256,896]{1,0:T(8,128)(2,1)} collective-permute-done((bf16[256,896]{1,0:T(8,128)(2,1)S(1)}, bf16[256,896]{1,0:T(8,128)(2,1)}, u32[]{:S(2)}, u32[]{:S(2)}) %collective-permute-start.14) | collective-permute-done | bytes 458784 | tf_op jit(solution)/shard_map/ppermute | solution.py:28
  97.3 6.6 %collective-permute-start.17 = (bf16[256,896]{1,0:T(8,128)(2,1)}, bf16[256,896]{1,0:T(8,128)(2,1)S(1)}, u32[]{:S(2)}, u32[]{:S(2)}) collective-permute-start(bf16[256,896]{1,0:T(8,128)(2,1)} %collective-permute-done.16.refs_3_), channel_id=1, source_target_pairs={{0,28},{1,29},{2,30},{3,31},{4,0},{5,1},{6,2},{7,3},{8,4},{9,5},{1... | collective-permute-start | bytes 1376264 | tf_op jit(solution)/shard_map/ppermute | solution.py:28
  103.9 16.1 %collective-permute-done.9.refs_1_ = bf16[256,896]{1,0:T(8,128)(2,1)} collective-permute-done((bf16[256,896]{1,0:T(8,128)(2,1)S(1)}, bf16[256,896]{1,0:T(8,128)(2,1)}, u32[]{:S(2)}, u32[]{:S(2)}) %collective-permute-start.9) | collective-permute-done | bytes 458784 | tf_op jit(solution)/shard_map/ppermute | solution.py:28
  120.0 7.1 %collective-permute-start.10 = (bf16[256,896]{1,0:T(8,128)(2,1)}, bf16[256,896]{1,0:T(8,128)(2,1)S(1)}, u32[]{:S(2)}, u32[]{:S(2)}) collective-permute-start(bf16[256,896]{1,0:T(8,128)(2,1)} %collective-permute-done.9.refs_1_), channel_id=1, source_target_pairs={{0,28},{1,29},{2,30},{3,31},{4,0},{5,1},{6,2},{7,3},{8,4},{9,5},{1... | collective-permute-start | bytes 1376264 | tf_op jit(solution)/shard_map/ppermute | solution.py:28
  134.9 4.3 %place_rows.7.hid = bf16[5,256,512]{2,1,0:T(8,128)(2,1)S(1)} custom-call(s32[66]{0:T(128)S(1)} %concatenate.18.index.ix, f32[32,8,128]{2,1,0:T(8,128)S(1)} %all-to-all-done.meta, bf16[3840,512]{1,0:T(8,128)(2,1)S(1)} %pad_maximum_fusion.rows), custom_call_target="tpu_custom_call" | custom-call | flops 393216000 | bytes 2621440 | tf_op jit(solution)/shard_map/place_rows/pallas_call | solution.py:65
  139.3 4.0 %round_blocks.3 = (f32[512,896]{1,0:T(8,128)S(1)}, f32[32,1,128]{2,1,0:T(1,128)}) custom-call(s32[66]{0:T(128)S(1)} %concatenate.18.index.ix, bf16[5,256,512]{2,1,0:T(8,128)(2,1)S(1)} %place_rows.7.hid, bf16[512,896]{1,0:T(8,128)(2,1)S(1)} %bitcast.54, bf16[256,896]{1,0:T(8,128)(2,1)S(1)} %get-tuple-element.21.refs_0_, bf16[256,896]{1,0:T(8,128)(2,1)S(1)} %copy-done.7, ...), custom_call_target="tpu_custom_call" | custom-call | flops 2348810240 | bytes 7274496 | tf_op jit(solution)/shard_map/round_blocks/pallas_call | solution.py:132
  145.9 5.0 %round_blocks.4 = (f32[512,896]{1,0:T(8,128)S(1)}, f32[32,1,128]{2,1,0:T(1,128)}) custom-call(s32[66]{0:T(128)S(1)} %concatenate.18.index.ix, bf16[4,256,512]{2,1,0:T(8,128)(2,1)S(1)} %place_rows.6.hid, bf16[512,896]{1,0:T(8,128)(2,1)S(1)} %bitcast.55, ...), custom_call_target="tpu_custom_call", output_to_operand_aliasing={{0}: (7, {}), {1}: (8, {})} | custom-call | flops 1879048192 | bytes 6553600 | tf_op jit(solution)/shard_map/round_blocks/pallas_call | solution.py:132
  150.8 7.5 %collective-permute-done.10.refs_1_ = bf16[256,896]{1,0:T(8,128)(2,1)S(1)} collective-permute-done((bf16[256,896]{1,0:T(8,128)(2,1)}, bf16[256,896]{1,0:T(8,128)(2,1)S(1)}, u32[]{:S(2)}, u32[]{:S(2)}) %collective-permute-start.10) | collective-permute-done | bytes 458784 | tf_op jit(solution)/shard_map/ppermute | solution.py:28
  158.3 6.1 %collective-permute-start.11 = (bf16[256,896]{1,0:T(8,128)(2,1)S(1)}, bf16[256,896]{1,0:T(8,128)(2,1)S(1)}, u32[]{:S(2)}, u32[]{:S(2)}) collective-permute-start(bf16[256,896]{1,0:T(8,128)(2,1)S(1)} %collective-permute-done.10.refs_1_), channel_id=1, source_target_pairs={{0,28},{1,29},{2,30},{3,31},{4,0},{5,1},{6,2},{7,3},{8,4},{9,5},{1... | collective-permute-start | bytes 1376264 | tf_op jit(solution)/shard_map/ppermute | solution.py:28
  172.7 5.7 %collective-permute-start.19 = (bf16[128,896]{1,0:T(8,128)(2,1)S(1)}, bf16[128,896]{1,0:T(8,128)(2,1)S(1)}, u32[]{:S(2)}, u32[]{:S(2)}) collective-permute-start(bf16[128,896]{1,0:T(8,128)(2,1)S(1)} %slice.15), channel_id=1, source_target_pairs={{0,28},{1,29},{2,30},{3,31},{4,0},{5,1},{6,2},{7,3},{8,4},{9,5},{1... | collective-permute-start | bytes 688136 | tf_op jit(solution)/shard_map/ppermute | solution.py:28
  178.4 4.2 %round_blocks.5 = (f32[512,896]{1,0:T(8,128)S(1)}, f32[32,1,128]{2,1,0:T(1,128)}) custom-call(s32[66]{0:T(128)S(1)} %concatenate.18.index.ix, bf16[4,256,512]{2,1,0:T(8,128)(2,1)S(1)} %place_rows.5.hid, bf16[512,896]{1,0:T(8,128)(2,1)S(1)} %bitcast.56, ...), custom_call_target="tpu_custom_call", output_to_operand_aliasing={{0}: (7, {}), {1}: (8, {})} | custom-call | flops 1879048192 | bytes 6553600 | tf_op jit(solution)/shard_map/round_blocks/pallas_call | solution.py:132
  186.5 11.1 %all-to-all-start.1 = ((f32[32,1,128]{2,1,0:T(1,128)}), f32[32,1,128]{2,1,0:T(1,128)S(1)}, u32[]{:S(2)}, u32[]{:S(2)}) async-start(f32[32,1,128]{2,1,0:T(1,128)} %last_dots.1), calls=%async_computation.1 | async-start | bytes 32768 | tf_op jit(solution)/shard_map/all_to_all | solution.py:285
  199.9 6.8 %collective-permute-start.20 = (bf16[256,896]{1,0:T(8,128)(2,1)}, bf16[256,896]{1,0:T(8,128)(2,1)}, u32[]{:S(2)}, u32[]{:S(2)}) collective-permute-start(bf16[256,896]{1,0:T(8,128)(2,1)} %last_grads.3), channel_id=1, source_target_pairs={{0,480},{32,448},{64,416},{96,384},{128,352},{160,320},{192,288},{... | collective-permute-start | bytes 1376264 | tf_op jit(solution)/shard_map/ppermute | solution.py:283
  211.2 6.4 %collective-permute-done.20 = bf16[256,896]{1,0:T(8,128)(2,1)} collective-permute-done((bf16[256,896]{1,0:T(8,128)(2,1)}, bf16[256,896]{1,0:T(8,128)(2,1)}, u32[]{:S(2)}, u32[]{:S(2)}) %collective-permute-start.20) | collective-permute-done | bytes 458784 | tf_op jit(solution)/shard_map/ppermute | solution.py:283
  (77 shorter events, 49.6 us)
Async XLA Ops:
  0.6 27.7 %collective-permute-start.1 = (bf16[960,512]{1,0:T(8,128)(2,1)}, bf16[960,512]{1,0:T(8,128)(2,1)}, u32[]{:S(2)}, u32[]{:S(2)}) collective-permute-start(bf16[960,512]{1,0:T(8,128)(2,1)} %bitcast.58), channel_id=1, source_target_pairs={{0,2},{1,3},{2,0},{3,1},{4,6},{5,7},{6,4},{7,5},{8,10},{9,11},{10,... | collective-permute-start | bytes 2949128 | tf_op jit(solution)/shard_map/ppermute | solution.py:33
  5.0 23.3 %collective-permute-start.2 = (bf16[960,512]{1,0:T(8,128)(2,1)}, bf16[960,512]{1,0:T(8,128)(2,1)}, u32[]{:S(2)}, u32[]{:S(2)}) collective-permute-start(bf16[960,512]{1,0:T(8,128)(2,1)} %bitcast.59), channel_id=1, source_target_pairs={{0,1},{1,0},{2,3},{3,2},{4,5},{5,4},{6,7},{7,6},{8,9},{9,8},{10,11... | collective-permute-start | bytes 2949128 | tf_op jit(solution)/shard_map/ppermute | solution.py:33
  12.8 15.4 %collective-permute-start = (bf16[2,128,896]{2,1,0:T(8,128)(2,1)S(1)}, bf16[2,128,896]{2,1,0:T(8,128)(2,1)S(1)}, u32[]{:S(2)}, u32[]{:S(2)}) collective-permute-start(bf16[2,128,896]{2,1,0:T(8,128)(2,1)S(1)} %pad_maximum_fusion.1), channel_id=1, source_target_pairs={{0,1},{1,0},{2,3},{3,2},{4,5},{5,4},{6,7},{7,6},{8,9},{9,8},{10,11... | collective-permute-start | bytes 1376264 | tf_op jit(solution)/shard_map/ppermute | solution.py:33
  16.8 38.7 %all-to-all-start = ((f32[32,8,128]{2,1,0:T(8,128)}), f32[32,8,128]{2,1,0:T(8,128)S(1)}, u32[]{:S(2)}, u32[]{:S(2)}) async-start(f32[32,8,128]{2,1,0:T(8,128)} %broadcast_in_dim.32), calls=%async_computation | async-start | bytes 262144 | tf_op jit(solution)/shard_map/all_to_all | solution.py:248
  28.4 33.0 %collective-permute-start.12 = (bf16[256,896]{1,0:T(8,128)(2,1)S(1)}, bf16[256,896]{1,0:T(8,128)(2,1)S(1)}, u32[]{:S(2)}, u32[]{:S(2)}) collective-permute-start(bf16[256,896]{1,0:T(8,128)(2,1)S(1)} %get-tuple-element.21.refs_0_), channel_id=1, source_target_pairs={{0,4},{1,5},{2,6},{3,7},{4,8},{5,9},{6,10},{7,11},{8,12},{9,13},{1... | collective-permute-start | bytes 1376264 | tf_op jit(solution)/shard_map/ppermute | solution.py:28
  32.6 28.8 %collective-permute-start.13 = (bf16[256,896]{1,0:T(8,128)(2,1)S(1)}, bf16[256,896]{1,0:T(8,128)(2,1)S(1)}, u32[]{:S(2)}, u32[]{:S(2)}) collective-permute-start(bf16[256,896]{1,0:T(8,128)(2,1)S(1)} %get-tuple-element.21.refs_0_), channel_id=1, source_target_pairs={{0,28},{1,29},{2,30},{3,31},{4,0},{5,1},{6,2},{7,3},{8,4},{9,5},{1... | collective-permute-start | bytes 1376264 | tf_op jit(solution)/shard_map/ppermute | solution.py:28
  43.7 25.6 %collective-permute-start.4 = (bf16[256,896]{1,0:T(8,128)(2,1)S(1)}, bf16[256,896]{1,0:T(8,128)(2,1)S(1)}, u32[]{:S(2)}, u32[]{:S(2)}) collective-permute-start(bf16[256,896]{1,0:T(8,128)(2,1)S(1)} %get-tuple-element.20), channel_id=1, source_target_pairs={{0,2},{1,3},{2,4},{3,5},{4,6},{5,7},{6,8},{7,9},{8,10},{9,11},{10,... | collective-permute-start | bytes 1376264 | tf_op jit(solution)/shard_map/ppermute | solution.py:28
  45.7 28.7 %collective-permute-start.8 = (bf16[256,896]{1,0:T(8,128)(2,1)S(1)}, bf16[256,896]{1,0:T(8,128)(2,1)S(1)}, u32[]{:S(2)}, u32[]{:S(2)}) collective-permute-start(bf16[256,896]{1,0:T(8,128)(2,1)S(1)} %get-tuple-element.20), channel_id=1, source_target_pairs={{0,30},{1,31},{2,0},{3,1},{4,2},{5,3},{6,4},{7,5},{8,6},{9,7},{10,... | collective-permute-start | bytes 1376264 | tf_op jit(solution)/shard_map/ppermute | solution.py:28
  50.2 78.8 %collective-permute-start.3 = (bf16[960,512]{1,0:T(8,128)(2,1)}, bf16[960,512]{1,0:T(8,128)(2,1)}, u32[]{:S(2)}, u32[]{:S(2)}) collective-permute-start(bf16[960,512]{1,0:T(8,128)(2,1)} %collective-permute-done.1), channel_id=1, source_target_pairs={{0,1},{1,0},{2,3},{3,2},{4,5},{5,4},{6,7},{7,6},{8,9},{9,8},{10,11... | collective-permute-start | bytes 2949128 | tf_op jit(solution)/shard_map/ppermute | solution.py:33
  61.3 70.0 %copy-start.4 = (bf16[256,896]{1,0:T(8,128)(2,1)}, bf16[256,896]{1,0:T(8,128)(2,1)S(1)}, u32[]{:S(2)}) copy-start(bf16[256,896]{1,0:T(8,128)(2,1)S(1)} %collective-permute-done.13.refs_4_) | copy-start | bytes 1376260
  61.3 34.0 %collective-permute-start.14 = (bf16[256,896]{1,0:T(8,128)(2,1)S(1)}, bf16[256,896]{1,0:T(8,128)(2,1)}, u32[]{:S(2)}, u32[]{:S(2)}) collective-permute-start(bf16[256,896]{1,0:T(8,128)(2,1)S(1)} %collective-permute-done.12.refs_3_), channel_id=1, source_target_pairs={{0,4},{1,5},{2,6},{3,7},{4,8},{5,9},{6,10},{7,11},{8,12},{9,13},{1... | collective-permute-start | bytes 1376264 | tf_op jit(solution)/shard_map/ppermute | solution.py:28
  63.2 34.0 %collective-permute-start.16 = (bf16[256,896]{1,0:T(8,128)(2,1)S(1)}, bf16[256,896]{1,0:T(8,128)(2,1)}, u32[]{:S(2)}, u32[]{:S(2)}) collective-permute-start(bf16[256,896]{1,0:T(8,128)(2,1)S(1)} %collective-permute-done.13.refs_4_), channel_id=1, source_target_pairs={{0,28},{1,29},{2,30},{3,31},{4,0},{5,1},{6,2},{7,3},{8,4},{9,5},{1... | collective-permute-start | bytes 1376264 | tf_op jit(solution)/shard_map/ppermute | solution.py:28
  69.4 57.7 %collective-permute-start.5 = (bf16[256,896]{1,0:T(8,128)(2,1)S(1)}, bf16[256,896]{1,0:T(8,128)(2,1)}, u32[]{:S(2)}, u32[]{:S(2)}) collective-permute-start(bf16[256,896]{1,0:T(8,128)(2,1)S(1)} %collective-permute-done.4.refs_1_), channel_id=1, source_target_pairs={{0,4},{1,5},{2,6},{3,7},{4,8},{5,9},{6,10},{7,11},{8,12},{9,13},{1... | collective-permute-start | bytes 1376264 | tf_op jit(solution)/shard_map/ppermute | solution.py:28
  74.4 45.6 %collective-permute-start.9 = (bf16[256,896]{1,0:T(8,128)(2,1)S(1)}, bf16[256,896]{1,0:T(8,128)(2,1)}, u32[]{:S(2)}, u32[]{:S(2)}) collective-permute-start(bf16[256,896]{1,0:T(8,128)(2,1)S(1)} %collective-permute-done.8.refs_2_), channel_id=1, source_target_pairs={{0,28},{1,29},{2,30},{3,31},{4,0},{5,1},{6,2},{7,3},{8,4},{9,5},{1... | collective-permute-start | bytes 1376264 | tf_op jit(solution)/shard_map/ppermute | solution.py:28
  95.4 47.9 %collective-permute-start.15 = (bf16[256,896]{1,0:T(8,128)(2,1)}, bf16[256,896]{1,0:T(8,128)(2,1)S(1)}, u32[]{:S(2)}, u32[]{:S(2)}) collective-permute-start(bf16[256,896]{1,0:T(8,128)(2,1)} %collective-permute-done.14.refs_2_), channel_id=1, source_target_pairs={{0,4},{1,5},{2,6},{3,7},{4,8},{5,9},{6,10},{7,11},{8,12},{9,13},{1... | collective-permute-start | bytes 1376264 | tf_op jit(solution)/shard_map/ppermute | solution.py:28
  97.3 46.0 %collective-permute-start.17 = (bf16[256,896]{1,0:T(8,128)(2,1)}, bf16[256,896]{1,0:T(8,128)(2,1)S(1)}, u32[]{:S(2)}, u32[]{:S(2)}) collective-permute-start(bf16[256,896]{1,0:T(8,128)(2,1)} %collective-permute-done.16.refs_3_), channel_id=1, source_target_pairs={{0,28},{1,29},{2,30},{3,31},{4,0},{5,1},{6,2},{7,3},{8,4},{9,5},{1... | collective-permute-start | bytes 1376264 | tf_op jit(solution)/shard_map/ppermute | solution.py:28
  120.0 38.3 %collective-permute-start.10 = (bf16[256,896]{1,0:T(8,128)(2,1)}, bf16[256,896]{1,0:T(8,128)(2,1)S(1)}, u32[]{:S(2)}, u32[]{:S(2)}) collective-permute-start(bf16[256,896]{1,0:T(8,128)(2,1)} %collective-permute-done.9.refs_1_), channel_id=1, source_target_pairs={{0,28},{1,29},{2,30},{3,31},{4,0},{5,1},{6,2},{7,3},{8,4},{9,5},{1... | collective-permute-start | bytes 1376264 | tf_op jit(solution)/shard_map/ppermute | solution.py:28
  127.1 37.3 %collective-permute-start.6 = (bf16[256,896]{1,0:T(8,128)(2,1)}, bf16[256,896]{1,0:T(8,128)(2,1)S(1)}, u32[]{:S(2)}, u32[]{:S(2)}) collective-permute-start(bf16[256,896]{1,0:T(8,128)(2,1)} %collective-permute-done.5.refs_0_), channel_id=1, source_target_pairs={{0,4},{1,5},{2,6},{3,7},{4,8},{5,9},{6,10},{7,11},{8,12},{9,13},{1... | collective-permute-start | bytes 1376264 | tf_op jit(solution)/shard_map/ppermute | solution.py:28
  143.3 39.3 %collective-permute-start.18 = (bf16[128,896]{1,0:T(8,128)(2,1)S(1)}, bf16[128,896]{1,0:T(8,128)(2,1)S(1)}, u32[]{:S(2)}, u32[]{:S(2)}) collective-permute-start(bf16[128,896]{1,0:T(8,128)(2,1)S(1)} %slice.14), channel_id=1, source_target_pairs={{0,4},{1,5},{2,6},{3,7},{4,8},{5,9},{6,10},{7,11},{8,12},{9,13},{1... | collective-permute-start | bytes 688136 | tf_op jit(solution)/shard_map/ppermute | solution.py:28
  158.3 24.4 %collective-permute-start.11 = (bf16[256,896]{1,0:T(8,128)(2,1)S(1)}, bf16[256,896]{1,0:T(8,128)(2,1)S(1)}, u32[]{:S(2)}, u32[]{:S(2)}) collective-permute-start(bf16[256,896]{1,0:T(8,128)(2,1)S(1)} %collective-permute-done.10.refs_1_), channel_id=1, source_target_pairs={{0,28},{1,29},{2,30},{3,31},{4,0},{5,1},{6,2},{7,3},{8,4},{9,5},{1... | collective-permute-start | bytes 1376264 | tf_op jit(solution)/shard_map/ppermute | solution.py:28
  164.4 18.3 %collective-permute-start.7 = (bf16[256,896]{1,0:T(8,128)(2,1)S(1)}, bf16[256,896]{1,0:T(8,128)(2,1)S(1)}, u32[]{:S(2)}, u32[]{:S(2)}) collective-permute-start(bf16[256,896]{1,0:T(8,128)(2,1)S(1)} %collective-permute-done.6.refs_0_), channel_id=1, source_target_pairs={{0,4},{1,5},{2,6},{3,7},{4,8},{5,9},{6,10},{7,11},{8,12},{9,13},{1... | collective-permute-start | bytes 1376264 | tf_op jit(solution)/shard_map/ppermute | solution.py:28
  172.7 9.9 %collective-permute-start.19 = (bf16[128,896]{1,0:T(8,128)(2,1)S(1)}, bf16[128,896]{1,0:T(8,128)(2,1)S(1)}, u32[]{:S(2)}, u32[]{:S(2)}) collective-permute-start(bf16[128,896]{1,0:T(8,128)(2,1)S(1)} %slice.15), channel_id=1, source_target_pairs={{0,28},{1,29},{2,30},{3,31},{4,0},{5,1},{6,2},{7,3},{8,4},{9,5},{1... | collective-permute-start | bytes 688136 | tf_op jit(solution)/shard_map/ppermute | solution.py:28
  186.5 22.8 %all-to-all-start.1 = ((f32[32,1,128]{2,1,0:T(1,128)}), f32[32,1,128]{2,1,0:T(1,128)S(1)}, u32[]{:S(2)}, u32[]{:S(2)}) async-start(f32[32,1,128]{2,1,0:T(1,128)} %last_dots.1), calls=%async_computation.1 | async-start | bytes 32768 | tf_op jit(solution)/shard_map/all_to_all | solution.py:285
  199.9 17.7 %collective-permute-start.20 = (bf16[256,896]{1,0:T(8,128)(2,1)}, bf16[256,896]{1,0:T(8,128)(2,1)}, u32[]{:S(2)}, u32[]{:S(2)}) collective-permute-start(bf16[256,896]{1,0:T(8,128)(2,1)} %last_grads.3), channel_id=1, source_target_pairs={{0,480},{32,448},{64,416},{96,384},{128,352},{160,320},{192,288},{... | collective-permute-start | bytes 1376264 | tf_op jit(solution)/shard_map/ppermute | solution.py:283
  (10 other events, 193.7 us)

commit v3 on v2

--- a/solution.py
+++ b/solution.py
@@ -214,6 +214,50 @@
     )(which, placed, grads, *rows)
 
 
+def adam_kernel(which, kept, received, weight, first, second, weight_out, first_out, second_out):
+    summed = kept[...].astype(jnp.float32) + received[...].astype(jnp.float32)
+    held = weight[...].astype(jnp.float32)
+    first_new = beta_first * first[...].astype(jnp.float32) + (1.0 - beta_first) * summed
+    second_new = (
+        beta_second * second[...].astype(jnp.float32) + (1.0 - beta_second) * summed * summed
+    )
+    first_hat = first_new * (1.0 / (1.0 - beta_first**step_count))
+    second_hat = second_new * (1.0 / (1.0 - beta_second**step_count))
+    updated = held - learn_rate * (
+        first_hat / (jnp.sqrt(second_hat) + epsilon) + decay_rate * held
+    )
+    weight_out[...] = updated.astype(weight_out.dtype)
+    first_out[...] = first_new.astype(first_out.dtype)
+    second_out[...] = second_new.astype(second_out.dtype)
+
+
+def adam_step(which, kept, received, weight, first, second):
+    rows, width = kept.shape
+    steps = 4
+    tile = pl.BlockSpec((rows // steps, width), lambda i, ix: (i, 0))
+    return pl.pallas_call(
+        adam_kernel,
+        grid_spec=pltpu.PrefetchScalarGridSpec(
+            num_scalar_prefetch=1,
+            grid=(steps,),
+            in_specs=[
+                tile,
+                tile,
+                pl.BlockSpec((rows // steps, width), lambda i, ix: (ix[0] * steps + i, 0)),
+                tile,
+                tile,
+            ],
+            out_specs=[tile] * 3,
+        ),
+        out_shape=[jax.ShapeDtypeStruct(kept.shape, jnp.bfloat16)] * 3,
+        cost_estimate=pl.CostEstimate(
+            flops=30 * rows * width, bytes_accessed=16 * rows * width, transcendentals=2 * rows * width
+        ),
+        compiler_params=pltpu.CompilerParams(vmem_limit_bytes=VMEM_BYTES),
+        name="adam_step",
+    )(which, kept, received, weight, first, second)
+
+
 def shards(upstream, routes, gates, hidden_saved, down_weight, first_moment, second_moment):
     rows_in = upstream[0]
     route_dev = routes[0]
@@ -254,8 +298,7 @@
 
     def round_at(number, rows, grads, dots):
         start, stop = ROUNDS[number]
-        placed = place_rows(index, meta, hidden, start, stop)
-        return round_call(index, start, rows, placed, weight, grads, dots)
+        return round_call(index, start, rows, placed[start:stop], weight, grads, dots)
 
     d1 = step((diff, diff), 1)
     s1 = step((same, same), 2)
@@ -263,51 +306,42 @@
     hidden = jnp.concatenate([own_hidden, core_hidden, chip_hidden, far_hidden], axis=0)
     d2 = step(d1, 2)
     s2 = step(s1, 2, meta)
-    d3 = step(d2, 2)
+    placed = place_rows(index, meta, hidden, 0, 16)
+    d3 = step(d2, 2, placed)
+    grads, dots = round_at(0, [same, *d1, *s1], None, None)
     s3 = step(s2, 2)
-    grads, dots = round_at(0, [same, *d1, *s1], None, None)
     d4 = step(d3, 2)
     grads1, dots = round_at(1, [*d2, *s2], grads, dots)
-    ahead = tie((*s3,))
+    ahead = s3
     across = (send_chips(ahead[0][:tokens], 2), send_chips(ahead[1][tokens:], -2))
     grads, dots = round_at(2, [*d3, *s3], grads1, dots)
     start, stop = ROUNDS[3]
     last = [*d4, jnp.concatenate(across, axis=0)]
-    placed_last = place_rows(index, meta, hidden, start, stop)
+    placed_last = placed[start:stop]
 
     pipe_rank = lax.axis_index("pp")
     rank_count = lax.axis_size("pp")
     upper = (pipe_rank >= rank_count // 2).astype(jnp.int32)
     half_units = units // 2
     moving = last_grads(jnp.stack([1 - upper]), last, placed_last, grads)
-    moving = lax.ppermute(moving, "pp", [(i, rank_count - 1 - i) for i in range(rank_count)])
-    dots = last_dots(index, start, last, placed_last, weight, dots)
+    received = lax.ppermute(moving, "pp", [(i, rank_count - 1 - i) for i in range(rank_count)])
+    dots = last_dots(index, start, last, placed_last, weight, tie((dots, moving))[0])
     returned = lax.all_to_all(dots, "ep", split_axis=0, concat_axis=0, tiled=True)
     kept = last_grads(jnp.stack([upper]), last, placed_last, grads)
 
-    summed = kept.astype(jnp.float32) + moving.astype(jnp.float32)
-    weight_kept = lax.dynamic_slice(weight, (upper * half_units, 0), (half_units, part)).astype(
-        jnp.float32
-    )
-    first_new = beta_first * first_moment[0, 0].astype(jnp.float32) + (1.0 - beta_first) * summed
-    second_new = (
-        beta_second * second_moment[0, 0].astype(jnp.float32)
-        + (1.0 - beta_second) * summed * summed
-    )
-    first_hat = first_new / (1.0 - beta_first**step_count)
-    second_hat = second_new / (1.0 - beta_second**step_count)
-    new_weight = weight_kept - learn_rate * (
-        first_hat / (jnp.sqrt(second_hat) + epsilon) + decay_rate * weight_kept
-    )
-
+    new_weight, first_new, second_new = adam_step(
+        jnp.stack([upper]), kept, received, weight, first_moment[0, 0], second_moment[0, 0]
+    )
+
+    returned = tie((returned, new_weight))[0]
     totals = jnp.sum(returned.reshape(EXP, 8, tokens), axis=1)
     named = route_dev[:, :, None] == jnp.arange(EXP, dtype=jnp.int32)[None, None, :]
     gate_grad = jnp.sum(jnp.where(named, totals.T[:, None, :], 0.0), axis=2) / gate_dev
     return (
         gate_grad[None],
-        new_weight.astype(jnp.bfloat16)[None, None],
-        first_new.astype(jnp.bfloat16)[None, None],
-        second_new.astype(jnp.bfloat16)[None, None],
+        new_weight[None, None],
+        first_new[None, None],
+        second_new[None, None],
     )
 
 

time: 223 us -> 220 us (0.987)
  starting transfers between devices: 117 us -> 109 us
  waiting for transfers between devices: 56.6 us -> 61.1 us
  other arithmetic: 9.57 us -> 5.81 us
  local copies, waits for them, and re-layouts: 4.92 us -> 7.57 us
    ppermute x16, waiting for transfers between devices: 49.1 us -> 55.5 us  [send_chips(): lax.ppermute(block, 'ep', [(i, (i + 2 * hops) % count) for i in range(cou...]
    ppermute x1, waiting for transfers between devices: 6.43 us -> 0.01 us  [shards(): lax.ppermute(moving, 'pp', [(i, rank_count - 1 - i) for i in range(rank_c...]
    ppermute x16, starting transfers between devices: 69.6 us -> 64.3 us  [send_chips(): lax.ppermute(block, 'ep', [(i, (i + 2 * hops) % count) for i in range(cou...]
    all_to_all x1, waiting for transfers between devices: 1.12 us -> 5.6 us  [shards(): lax.all_to_all(dots, 'ep', split_axis=0, concat_axis=0, tiled=True)]
    broadcast_in_dim x1 -> x0, other arithmetic: 3.76 us -> none  [shards(): second_new.astype(jnp.bfloat16)[None, None]]
    pallas_call x0 -> x1, Pallas kernels: none -> 3.67 us  [adam_step(): pl.pallas_call(adam_kernel, grid_spec=pltpu.PrefetchScalarGridSpec(num_sc...]
    unnamed x23 -> x27, local copies, waits for them, and re-layouts: 2.61 us -> 4.93 us
    pallas_call x4 -> x1, Pallas kernels: 14.2 us -> 12.5 us  [place_rows(): pl.pallas_call(place_kernel, grid_spec=pltpu.PrefetchScalarGridSpec(num_s...]
  transfers between devices with their start and end apart: 23 -> 23, of which waited for: 7 -> 6; matrix products, arithmetic and copies ran while one was open for 4% -> 3% of each run, Pallas kernels for 13% -> 15%
where the time goes in v3:
time: 220 us; the launch traced here: 219 us
  starting transfers between devices  109 us (50%)
  waiting for transfers between devices  61.1 us (28%)
  Pallas kernels  34 us (15%)
  local copies, waits for them, and re-layouts  7.57 us (3%)
  other arithmetic  5.81 us (3%)
    ppermute x16, starting transfers between devices, send_chips(): lax.ppermute(block, 'ep', [(i, (i + 2 * hops) % count) for i in range(cou...  64.3 us
    ppermute x16, waiting for transfers between devices, send_chips(): lax.ppermute(block, 'ep', [(i, (i + 2 * hops) % count) for i in range(cou...  55.5 us
    ppermute x4, starting transfers between devices, swap_bits(): return lax.ppermute(block, 'ep', [(i, i ^ bits) for i in range(count)])  17.3 us
    pallas_call x3, Pallas kernels, round_call(): pl.pallas_call(kernel, grid_spec=pltpu.PrefetchScalarGridSpec(num_scalar_...  12.9 us
    pallas_call x1, Pallas kernels, place_rows(): pl.pallas_call(place_kernel, grid_spec=pltpu.PrefetchScalarGridSpec(num_s...  12.5 us
    all_to_all x1, starting transfers between devices, shards(): meta = lax.all_to_all(meta, 'ep', split_axis=0, concat_axis=0, tiled=True)  11.4 us
    all_to_all x1, starting transfers between devices, shards(): lax.all_to_all(dots, 'ep', split_axis=0, concat_axis=0, tiled=True)  9.13 us
    ppermute x1, starting transfers between devices, shards(): lax.ppermute(moving, 'pp', [(i, rank_count - 1 - i) for i in range(rank_c...  6.83 us
  transfers between devices with their start and end apart: 23, of which 6 were waited for; matrix products, arithmetic and copies ran while one was open for 3% of the time, Pallas kernels for 15%

profile of v3, /device:TPU:1, one launch (start us, length us, event | category | flops | bytes accessed | tf_op | source)
XLA Modules:
  0.0 218.6 jit_solution(5767948597616415380)
XLA Ops:
  0.6 4.4 %collective-permute-start.1 = (bf16[960,512]{1,0:T(8,128)(2,1)}, bf16[960,512]{1,0:T(8,128)(2,1)}, u32[]{:S(2)}, u32[]{:S(2)}) collective-permute-start(bf16[960,512]{1,0:T(8,128)(2,1)} %bitcast.37), channel_id=1, source_target_pairs={{0,2},{1,3},{2,0},{3,1},{4,6},{5,7},{6,4},{7,5},{8,10},{9,11},{10,... | collective-permute-start | bytes 2949128 | tf_op jit(solution)/shard_map/ppermute | solution.py:33
  5.0 6.3 %collective-permute-start.2 = (bf16[960,512]{1,0:T(8,128)(2,1)}, bf16[960,512]{1,0:T(8,128)(2,1)}, u32[]{:S(2)}, u32[]{:S(2)}) collective-permute-start(bf16[960,512]{1,0:T(8,128)(2,1)} %bitcast.38), channel_id=1, source_target_pairs={{0,1},{1,0},{2,3},{3,2},{4,5},{5,4},{6,7},{7,6},{8,9},{9,8},{10,11... | collective-permute-start | bytes 2949128 | tf_op jit(solution)/shard_map/ppermute | solution.py:33
  16.8 11.4 %all-to-all-start = ((f32[32,8,128]{2,1,0:T(8,128)}), f32[32,8,128]{2,1,0:T(8,128)S(1)}, u32[]{:S(2)}, u32[]{:S(2)}) async-start(f32[32,8,128]{2,1,0:T(8,128)} %broadcast_in_dim.32), calls=%async_computation | async-start | bytes 262144 | tf_op jit(solution)/shard_map/all_to_all | solution.py:292
  28.4 4.2 %collective-permute-start.12 = (bf16[256,896]{1,0:T(8,128)(2,1)S(1)}, bf16[256,896]{1,0:T(8,128)(2,1)S(1)}, u32[]{:S(2)}, u32[]{:S(2)}) collective-permute-start(bf16[256,896]{1,0:T(8,128)(2,1)S(1)} %get-tuple-element.28.refs_0_), channel_id=1, source_target_pairs={{0,4},{1,5},{2,6},{3,7},{4,8},{5,9},{6,10},{7,11},{8,12},{9,13},{1... | collective-permute-start | bytes 1376264 | tf_op jit(solution)/shard_map/ppermute | solution.py:28
  32.6 11.2 %collective-permute-start.13 = (bf16[256,896]{1,0:T(8,128)(2,1)S(1)}, bf16[256,896]{1,0:T(8,128)(2,1)S(1)}, u32[]{:S(2)}, u32[]{:S(2)}) collective-permute-start(bf16[256,896]{1,0:T(8,128)(2,1)S(1)} %get-tuple-element.28.refs_0_), channel_id=1, source_target_pairs={{0,28},{1,29},{2,30},{3,31},{4,0},{5,1},{6,2},{7,3},{8,4},{9,5},{1... | collective-permute-start | bytes 1376264 | tf_op jit(solution)/shard_map/ppermute | solution.py:28
  43.7 4.6 %collective-permute-start.3 = (bf16[960,512]{1,0:T(8,128)(2,1)}, bf16[960,512]{1,0:T(8,128)(2,1)}, u32[]{:S(2)}, u32[]{:S(2)}) collective-permute-start(bf16[960,512]{1,0:T(8,128)(2,1)} %collective-permute-done.1), channel_id=1, source_target_pairs={{0,1},{1,0},{2,3},{3,2},{4,5},{5,4},{6,7},{7,6},{8,9},{9,8},{10,11... | collective-permute-start | bytes 2949128 | tf_op jit(solution)/shard_map/ppermute | solution.py:33
  50.3 4.6 %collective-permute-start.6 = (bf16[256,896]{1,0:T(8,128)(2,1)S(1)}, bf16[256,896]{1,0:T(8,128)(2,1)S(1)}, u32[]{:S(2)}, u32[]{:S(2)}) collective-permute-start(bf16[256,896]{1,0:T(8,128)(2,1)S(1)} %get-tuple-element.25), channel_id=1, source_target_pairs={{0,30},{1,31},{2,0},{3,1},{4,2},{5,3},{6,4},{7,5},{8,6},{9,7},{10,... | collective-permute-start | bytes 1376264 | tf_op jit(solution)/shard_map/ppermute | solution.py:28
  54.9 6.4 %collective-permute-done.12.refs_3_ = bf16[256,896]{1,0:T(8,128)(2,1)S(1)} collective-permute-done((bf16[256,896]{1,0:T(8,128)(2,1)S(1)}, bf16[256,896]{1,0:T(8,128)(2,1)S(1)}, u32[]{:S(2)}, u32[]{:S(2)}) %collective-permute-start.12) | collective-permute-done | bytes 458784 | tf_op jit(solution)/shard_map/ppermute | solution.py:28
  63.9 5.6 %collective-permute-start.17 = (bf16[256,896]{1,0:T(8,128)(2,1)S(1)}, bf16[256,896]{1,0:T(8,128)(2,1)}, u32[]{:S(2)}, u32[]{:S(2)}) collective-permute-start(bf16[256,896]{1,0:T(8,128)(2,1)S(1)} %collective-permute-done.13.refs_4_), channel_id=1, source_target_pairs={{0,28},{1,29},{2,30},{3,31},{4,0},{5,1},{6,2},{7,3},{8,4},{9,5},{1... | collective-permute-start | bytes 1376264 | tf_op jit(solution)/shard_map/ppermute | solution.py:28
  77.2 22.0 %collective-permute-done.14.refs_2_ = bf16[256,896]{1,0:T(8,128)(2,1)} collective-permute-done((bf16[256,896]{1,0:T(8,128)(2,1)S(1)}, bf16[256,896]{1,0:T(8,128)(2,1)}, u32[]{:S(2)}, u32[]{:S(2)}) %collective-permute-start.14) | collective-permute-done | bytes 458784 | tf_op jit(solution)/shard_map/ppermute | solution.py:28
  101.1 5.5 %collective-permute-start.18 = (bf16[256,896]{1,0:T(8,128)(2,1)}, bf16[256,896]{1,0:T(8,128)(2,1)S(1)}, u32[]{:S(2)}, u32[]{:S(2)}) collective-permute-start(bf16[256,896]{1,0:T(8,128)(2,1)} %collective-permute-done.17.refs_3_), channel_id=1, source_target_pairs={{0,28},{1,29},{2,30},{3,31},{4,0},{5,1},{6,2},{7,3},{8,4},{9,5},{1... | collective-permute-start | bytes 1376264 | tf_op jit(solution)/shard_map/ppermute | solution.py:28
  108.9 12.5 %place_rows.1 = bf16[16,256,512]{2,1,0:T(8,128)(2,1)S(1)} custom-call(s32[66]{0:T(128)S(1)} %concatenate.18.index.ix, f32[32,8,128]{2,1,0:T(8,128)S(1)} %all-to-all-done.meta, bf16[3840,512]{1,0:T(8,128)(2,1)S(1)} %pad_maximum_fusion.rows), custom_call_target="tpu_custom_call" | custom-call | flops 1258291200 | bytes 8388608 | tf_op jit(solution)/shard_map/place_rows/pallas_call | solution.py:65
  124.3 3.5 %collective-permute-start.8 = (bf16[256,896]{1,0:T(8,128)(2,1)S(1)}, bf16[256,896]{1,0:T(8,128)(2,1)S(1)}, u32[]{:S(2)}, u32[]{:S(2)}) collective-permute-start(bf16[256,896]{1,0:T(8,128)(2,1)S(1)} %collective-permute-done.5.refs_0_), channel_id=1, source_target_pairs={{0,4},{1,5},{2,6},{3,7},{4,8},{5,9},{6,10},{7,11},{8,12},{9,13},{1... | collective-permute-start | bytes 1376264 | tf_op jit(solution)/shard_map/ppermute | solution.py:28
  130.8 4.0 %round_blocks.3 = (f32[512,896]{1,0:T(8,128)S(1)}, f32[32,1,128]{2,1,0:T(1,128)}) custom-call(s32[66]{0:T(128)S(1)} %concatenate.18.index.ix, bf16[5,256,512]{2,1,0:T(8,128)(2,1)S(1)} %slice.39.hid, bf16[512,896]{1,0:T(8,128)(2,1)S(1)} %bitcast.30, bf16[256,896]{1,0:T(8,128)(2,1)S(1)} %get-tuple-element.28.refs_0_, bf16[256,896]{1,0:T(8,128)(2,1)S(1)} %copy-done.9, ...), custom_call_target="tpu_custom_call" | custom-call | flops 2348810240 | bytes 7274496 | tf_op jit(solution)/shard_map/round_blocks/pallas_call | solution.py:132
  137.0 13.9 %collective-permute-done.10.refs_1_ = bf16[256,896]{1,0:T(8,128)(2,1)S(1)} collective-permute-done((bf16[256,896]{1,0:T(8,128)(2,1)S(1)}, bf16[256,896]{1,0:T(8,128)(2,1)S(1)}, u32[]{:S(2)}, u32[]{:S(2)}) %collective-permute-start.10) | collective-permute-done | bytes 458784 | tf_op jit(solution)/shard_map/ppermute | solution.py:28
  150.9 6.2 %collective-permute-start.11 = (bf16[256,896]{1,0:T(8,128)(2,1)S(1)}, bf16[256,896]{1,0:T(8,128)(2,1)S(1)}, u32[]{:S(2)}, u32[]{:S(2)}) collective-permute-start(bf16[256,896]{1,0:T(8,128)(2,1)S(1)} %collective-permute-done.10.refs_1_), channel_id=1, source_target_pairs={{0,28},{1,29},{2,30},{3,31},{4,0},{5,1},{6,2},{7,3},{8,4},{9,5},{1... | collective-permute-start | bytes 1376264 | tf_op jit(solution)/shard_map/ppermute | solution.py:28
  159.0 4.7 %round_blocks.4 = (f32[512,896]{1,0:T(8,128)S(1)}, f32[32,1,128]{2,1,0:T(1,128)}) custom-call(s32[66]{0:T(128)S(1)} %concatenate.18.index.ix, bf16[4,256,512]{2,1,0:T(8,128)(2,1)S(1)} %get-tuple-element.44.hid, bf16[512,896]{1,0:T(8,128)(2,1)S(1)} %bitcast.31, ...), custom_call_target="tpu_custom_call", output_to_operand_aliasing={{0}: (7, {}), {1}: (8, {})} | custom-call | flops 1879048192 | bytes 6553600 | tf_op jit(solution)/shard_map/round_blocks/pallas_call | solution.py:132
  163.8 5.5 %collective-permute-start.19 = (bf16[128,896]{1,0:T(8,128)(2,1)S(1)}, bf16[128,896]{1,0:T(8,128)(2,1)S(1)}, u32[]{:S(2)}, u32[]{:S(2)}) collective-permute-start(bf16[128,896]{1,0:T(8,128)(2,1)S(1)} %slice.36), channel_id=1, source_target_pairs={{0,28},{1,29},{2,30},{3,31},{4,0},{5,1},{6,2},{7,3},{8,4},{9,5},{1... | collective-permute-start | bytes 688136 | tf_op jit(solution)/shard_map/ppermute | solution.py:28
  169.3 4.2 %round_blocks.5 = (f32[512,896]{1,0:T(8,128)S(1)}, f32[32,1,128]{2,1,0:T(1,128)}) custom-call(s32[66]{0:T(128)S(1)} %concatenate.18.index.ix, bf16[4,256,512]{2,1,0:T(8,128)(2,1)S(1)} %get-tuple-element.45.hid, bf16[512,896]{1,0:T(8,128)(2,1)S(1)} %bitcast.32, ...), custom_call_target="tpu_custom_call", output_to_operand_aliasing={{0}: (7, {}), {1}: (8, {})} | custom-call | flops 1879048192 | bytes 6553600 | tf_op jit(solution)/shard_map/round_blocks/pallas_call | solution.py:132
  173.5 11.0 %collective-permute-done.19 = bf16[128,896]{1,0:T(8,128)(2,1)S(1)} collective-permute-done((bf16[128,896]{1,0:T(8,128)(2,1)S(1)}, bf16[128,896]{1,0:T(8,128)(2,1)S(1)}, u32[]{:S(2)}, u32[]{:S(2)}) %collective-permute-start.19) | collective-permute-done | bytes 229408 | tf_op jit(solution)/shard_map/ppermute | solution.py:28
  185.9 6.8 %collective-permute-start.20 = (bf16[256,896]{1,0:T(8,128)(2,1)}, bf16[256,896]{1,0:T(8,128)(2,1)}, u32[]{:S(2)}, u32[]{:S(2)}) collective-permute-start(bf16[256,896]{1,0:T(8,128)(2,1)} %last_grads.2), channel_id=1, source_target_pairs={{0,480},{32,448},{64,416},{96,384},{128,352},{160,320},{192,288},{... | collective-permute-start | bytes 1376264 | tf_op jit(solution)/shard_map/ppermute | solution.py:327
  195.8 9.1 %all-to-all-start.1 = ((f32[32,1,128]{2,1,0:T(1,128)}), f32[32,1,128]{2,1,0:T(1,128)S(1)}, u32[]{:S(2)}, u32[]{:S(2)}) async-start(f32[32,1,128]{2,1,0:T(1,128)} %last_dots.1), calls=%async_computation.1 | async-start | bytes 32768 | tf_op jit(solution)/shard_map/all_to_all | solution.py:329
  207.4 3.7 %adam_step.1 = (bf16[256,896]{1,0:T(8,128)(2,1)}, bf16[256,896]{1,0:T(8,128)(2,1)}, bf16[256,896]{1,0:T(8,128)(2,1)}) custom-call(s32[1]{0:T(128)} %bitcast.12.ix.which, bf16[256,896]{1,0:T(8,128)(2,1)S(1)} %last_grads.3.kept, bf16[256,896]{1,0:T(8,128)(2,1)} %collective-permute-done.20.received, bf16[512,896]{1,0:T(8,128)(2,1)S(1)} %bitcast.34, ...), custom_call_target="tpu_custom_call" | custom-call | flops 6881280 | bytes 3670016 | tf_op jit(solution)/shard_map/adam_step/pallas_call | solution.py:238
  211.1 5.6 %all-to-all-done.1 = f32[32,1,128]{2,1,0:T(1,128)S(1)} async-done(((f32[32,1,128]{2,1,0:T(1,128)}), f32[32,1,128]{2,1,0:T(1,128)S(1)}, u32[]{:S(2)}, u32[]{:S(2)}) %all-to-all-start.1) | async-done | bytes 16416 | tf_op jit(solution)/shard_map/all_to_all | solution.py:329
  (81 shorter events, 40.7 us)
Async XLA Ops:
  0.6 47.8 %copy-start.12 = (s32[16]{0:T(128)S(1)}, s32[16]{0:T(128)}, u32[]{:S(2)}) copy-start(s32[16]{0:T(128)} %constant.101.clone) | copy-start | bytes 196
  0.6 27.7 %collective-permute-start.1 = (bf16[960,512]{1,0:T(8,128)(2,1)}, bf16[960,512]{1,0:T(8,128)(2,1)}, u32[]{:S(2)}, u32[]{:S(2)}) collective-permute-start(bf16[960,512]{1,0:T(8,128)(2,1)} %bitcast.37), channel_id=1, source_target_pairs={{0,2},{1,3},{2,0},{3,1},{4,6},{5,7},{6,4},{7,5},{8,10},{9,11},{10,... | collective-permute-start | bytes 2949128 | tf_op jit(solution)/shard_map/ppermute | solution.py:33
  5.0 23.3 %collective-permute-start.2 = (bf16[960,512]{1,0:T(8,128)(2,1)}, bf16[960,512]{1,0:T(8,128)(2,1)}, u32[]{:S(2)}, u32[]{:S(2)}) collective-permute-start(bf16[960,512]{1,0:T(8,128)(2,1)} %bitcast.38), channel_id=1, source_target_pairs={{0,1},{1,0},{2,3},{3,2},{4,5},{5,4},{6,7},{7,6},{8,9},{9,8},{10,11... | collective-permute-start | bytes 2949128 | tf_op jit(solution)/shard_map/ppermute | solution.py:33
  12.8 15.4 %collective-permute-start = (bf16[2,128,896]{2,1,0:T(8,128)(2,1)S(1)}, bf16[2,128,896]{2,1,0:T(8,128)(2,1)S(1)}, u32[]{:S(2)}, u32[]{:S(2)}) collective-permute-start(bf16[2,128,896]{2,1,0:T(8,128)(2,1)S(1)} %pad_maximum_fusion.1), channel_id=1, source_target_pairs={{0,1},{1,0},{2,3},{3,2},{4,5},{5,4},{6,7},{7,6},{8,9},{9,8},{10,11... | collective-permute-start | bytes 1376264 | tf_op jit(solution)/shard_map/ppermute | solution.py:33
  16.8 38.1 %all-to-all-start = ((f32[32,8,128]{2,1,0:T(8,128)}), f32[32,8,128]{2,1,0:T(8,128)S(1)}, u32[]{:S(2)}, u32[]{:S(2)}) async-start(f32[32,8,128]{2,1,0:T(8,128)} %broadcast_in_dim.32), calls=%async_computation | async-start | bytes 262144 | tf_op jit(solution)/shard_map/all_to_all | solution.py:292
  28.4 33.0 %collective-permute-start.12 = (bf16[256,896]{1,0:T(8,128)(2,1)S(1)}, bf16[256,896]{1,0:T(8,128)(2,1)S(1)}, u32[]{:S(2)}, u32[]{:S(2)}) collective-permute-start(bf16[256,896]{1,0:T(8,128)(2,1)S(1)} %get-tuple-element.28.refs_0_), channel_id=1, source_target_pairs={{0,4},{1,5},{2,6},{3,7},{4,8},{5,9},{6,10},{7,11},{8,12},{9,13},{1... | collective-permute-start | bytes 1376264 | tf_op jit(solution)/shard_map/ppermute | solution.py:28
  32.6 28.8 %collective-permute-start.13 = (bf16[256,896]{1,0:T(8,128)(2,1)S(1)}, bf16[256,896]{1,0:T(8,128)(2,1)S(1)}, u32[]{:S(2)}, u32[]{:S(2)}) collective-permute-start(bf16[256,896]{1,0:T(8,128)(2,1)S(1)} %get-tuple-element.28.refs_0_), channel_id=1, source_target_pairs={{0,28},{1,29},{2,30},{3,31},{4,0},{5,1},{6,2},{7,3},{8,4},{9,5},{1... | collective-permute-start | bytes 1376264 | tf_op jit(solution)/shard_map/ppermute | solution.py:28
  43.7 62.9 %collective-permute-start.3 = (bf16[960,512]{1,0:T(8,128)(2,1)}, bf16[960,512]{1,0:T(8,128)(2,1)}, u32[]{:S(2)}, u32[]{:S(2)}) collective-permute-start(bf16[960,512]{1,0:T(8,128)(2,1)} %collective-permute-done.1), channel_id=1, source_target_pairs={{0,1},{1,0},{2,3},{3,2},{4,5},{5,4},{6,7},{7,6},{8,9},{9,8},{10,11... | collective-permute-start | bytes 2949128 | tf_op jit(solution)/shard_map/ppermute | solution.py:33
  48.4 21.4 %collective-permute-start.4 = (bf16[256,896]{1,0:T(8,128)(2,1)S(1)}, bf16[256,896]{1,0:T(8,128)(2,1)S(1)}, u32[]{:S(2)}, u32[]{:S(2)}) collective-permute-start(bf16[256,896]{1,0:T(8,128)(2,1)S(1)} %get-tuple-element.25), channel_id=1, source_target_pairs={{0,2},{1,3},{2,4},{3,5},{4,6},{5,7},{6,8},{7,9},{8,10},{9,11},{10,... | collective-permute-start | bytes 1376264 | tf_op jit(solution)/shard_map/ppermute | solution.py:28
  50.3 23.6 %collective-permute-start.6 = (bf16[256,896]{1,0:T(8,128)(2,1)S(1)}, bf16[256,896]{1,0:T(8,128)(2,1)S(1)}, u32[]{:S(2)}, u32[]{:S(2)}) collective-permute-start(bf16[256,896]{1,0:T(8,128)(2,1)S(1)} %get-tuple-element.25), channel_id=1, source_target_pairs={{0,30},{1,31},{2,0},{3,1},{4,2},{5,3},{6,4},{7,5},{8,6},{9,7},{10,... | collective-permute-start | bytes 1376264 | tf_op jit(solution)/shard_map/ppermute | solution.py:28
  61.3 37.9 %collective-permute-start.14 = (bf16[256,896]{1,0:T(8,128)(2,1)S(1)}, bf16[256,896]{1,0:T(8,128)(2,1)}, u32[]{:S(2)}, u32[]{:S(2)}) collective-permute-start(bf16[256,896]{1,0:T(8,128)(2,1)S(1)} %collective-permute-done.12.refs_3_), channel_id=1, source_target_pairs={{0,4},{1,5},{2,6},{3,7},{4,8},{5,9},{6,10},{7,11},{8,12},{9,13},{1... | collective-permute-start | bytes 1376264 | tf_op jit(solution)/shard_map/ppermute | solution.py:28
  63.9 37.2 %collective-permute-start.17 = (bf16[256,896]{1,0:T(8,128)(2,1)S(1)}, bf16[256,896]{1,0:T(8,128)(2,1)}, u32[]{:S(2)}, u32[]{:S(2)}) collective-permute-start(bf16[256,896]{1,0:T(8,128)(2,1)S(1)} %collective-permute-done.13.refs_4_), channel_id=1, source_target_pairs={{0,28},{1,29},{2,30},{3,31},{4,0},{5,1},{6,2},{7,3},{8,4},{9,5},{1... | collective-permute-start | bytes 1376264 | tf_op jit(solution)/shard_map/ppermute | solution.py:28
  69.8 51.7 %collective-permute-start.5 = (bf16[256,896]{1,0:T(8,128)(2,1)S(1)}, bf16[256,896]{1,0:T(8,128)(2,1)S(1)}, u32[]{:S(2)}, u32[]{:S(2)}) collective-permute-start(bf16[256,896]{1,0:T(8,128)(2,1)S(1)} %collective-permute-done.4.refs_1_), channel_id=1, source_target_pairs={{0,4},{1,5},{2,6},{3,7},{4,8},{5,9},{6,10},{7,11},{8,12},{9,13},{1... | collective-permute-start | bytes 1376264 | tf_op jit(solution)/shard_map/ppermute | solution.py:28
  73.9 47.6 %collective-permute-start.7 = (bf16[256,896]{1,0:T(8,128)(2,1)S(1)}, bf16[256,896]{1,0:T(8,128)(2,1)S(1)}, u32[]{:S(2)}, u32[]{:S(2)}) collective-permute-start(bf16[256,896]{1,0:T(8,128)(2,1)S(1)} %collective-permute-done.6.refs_2_), channel_id=1, source_target_pairs={{0,28},{1,29},{2,30},{3,31},{4,0},{5,1},{6,2},{7,3},{8,4},{9,5},{1... | collective-permute-start | bytes 1376264 | tf_op jit(solution)/shard_map/ppermute | solution.py:28
  99.2 35.8 %collective-permute-start.15 = (bf16[256,896]{1,0:T(8,128)(2,1)}, bf16[256,896]{1,0:T(8,128)(2,1)S(1)}, u32[]{:S(2)}, u32[]{:S(2)}) collective-permute-start(bf16[256,896]{1,0:T(8,128)(2,1)} %collective-permute-done.14.refs_2_), channel_id=1, source_target_pairs={{0,4},{1,5},{2,6},{3,7},{4,8},{5,9},{6,10},{7,11},{8,12},{9,13},{1... | collective-permute-start | bytes 1376264 | tf_op jit(solution)/shard_map/ppermute | solution.py:28
  101.1 62.6 %collective-permute-start.18 = (bf16[256,896]{1,0:T(8,128)(2,1)}, bf16[256,896]{1,0:T(8,128)(2,1)S(1)}, u32[]{:S(2)}, u32[]{:S(2)}) collective-permute-start(bf16[256,896]{1,0:T(8,128)(2,1)} %collective-permute-done.17.refs_3_), channel_id=1, source_target_pairs={{0,28},{1,29},{2,30},{3,31},{4,0},{5,1},{6,2},{7,3},{8,4},{9,5},{1... | collective-permute-start | bytes 1376264 | tf_op jit(solution)/shard_map/ppermute | solution.py:28
  121.5 29.3 %collective-permute-start.10 = (bf16[256,896]{1,0:T(8,128)(2,1)S(1)}, bf16[256,896]{1,0:T(8,128)(2,1)S(1)}, u32[]{:S(2)}, u32[]{:S(2)}) collective-permute-start(bf16[256,896]{1,0:T(8,128)(2,1)S(1)} %collective-permute-done.7.refs_1_), channel_id=1, source_target_pairs={{0,28},{1,29},{2,30},{3,31},{4,0},{5,1},{6,2},{7,3},{8,4},{9,5},{1... | collective-permute-start | bytes 1376264 | tf_op jit(solution)/shard_map/ppermute | solution.py:28
  124.3 32.8 %collective-permute-start.8 = (bf16[256,896]{1,0:T(8,128)(2,1)S(1)}, bf16[256,896]{1,0:T(8,128)(2,1)S(1)}, u32[]{:S(2)}, u32[]{:S(2)}) collective-permute-start(bf16[256,896]{1,0:T(8,128)(2,1)S(1)} %collective-permute-done.5.refs_0_), channel_id=1, source_target_pairs={{0,4},{1,5},{2,6},{3,7},{4,8},{5,9},{6,10},{7,11},{8,12},{9,13},{1... | collective-permute-start | bytes 1376264 | tf_op jit(solution)/shard_map/ppermute | solution.py:28
  135.0 38.4 %collective-permute-start.16 = (bf16[128,896]{1,0:T(8,128)(2,1)S(1)}, bf16[128,896]{1,0:T(8,128)(2,1)S(1)}, u32[]{:S(2)}, u32[]{:S(2)}) collective-permute-start(bf16[128,896]{1,0:T(8,128)(2,1)S(1)} %slice.35), channel_id=1, source_target_pairs={{0,4},{1,5},{2,6},{3,7},{4,8},{5,9},{6,10},{7,11},{8,12},{9,13},{1... | collective-permute-start | bytes 688136 | tf_op jit(solution)/shard_map/ppermute | solution.py:28
  150.9 33.7 %collective-permute-start.11 = (bf16[256,896]{1,0:T(8,128)(2,1)S(1)}, bf16[256,896]{1,0:T(8,128)(2,1)S(1)}, u32[]{:S(2)}, u32[]{:S(2)}) collective-permute-start(bf16[256,896]{1,0:T(8,128)(2,1)S(1)} %collective-permute-done.10.refs_1_), channel_id=1, source_target_pairs={{0,28},{1,29},{2,30},{3,31},{4,0},{5,1},{6,2},{7,3},{8,4},{9,5},{1... | collective-permute-start | bytes 1376264 | tf_op jit(solution)/shard_map/ppermute | solution.py:28
  157.1 27.5 %collective-permute-start.9 = (bf16[256,896]{1,0:T(8,128)(2,1)S(1)}, bf16[256,896]{1,0:T(8,128)(2,1)S(1)}, u32[]{:S(2)}, u32[]{:S(2)}) collective-permute-start(bf16[256,896]{1,0:T(8,128)(2,1)S(1)} %collective-permute-done.8.refs_0_), channel_id=1, source_target_pairs={{0,4},{1,5},{2,6},{3,7},{4,8},{5,9},{6,10},{7,11},{8,12},{9,13},{1... | collective-permute-start | bytes 1376264 | tf_op jit(solution)/shard_map/ppermute | solution.py:28
  163.8 20.7 %collective-permute-start.19 = (bf16[128,896]{1,0:T(8,128)(2,1)S(1)}, bf16[128,896]{1,0:T(8,128)(2,1)S(1)}, u32[]{:S(2)}, u32[]{:S(2)}) collective-permute-start(bf16[128,896]{1,0:T(8,128)(2,1)S(1)} %slice.36), channel_id=1, source_target_pairs={{0,28},{1,29},{2,30},{3,31},{4,0},{5,1},{6,2},{7,3},{8,4},{9,5},{1... | collective-permute-start | bytes 688136 | tf_op jit(solution)/shard_map/ppermute | solution.py:28
  185.9 20.6 %collective-permute-start.20 = (bf16[256,896]{1,0:T(8,128)(2,1)}, bf16[256,896]{1,0:T(8,128)(2,1)}, u32[]{:S(2)}, u32[]{:S(2)}) collective-permute-start(bf16[256,896]{1,0:T(8,128)(2,1)} %last_grads.2), channel_id=1, source_target_pairs={{0,480},{32,448},{64,416},{96,384},{128,352},{160,320},{192,288},{... | collective-permute-start | bytes 1376264 | tf_op jit(solution)/shard_map/ppermute | solution.py:327
  195.8 20.9 %all-to-all-start.1 = ((f32[32,1,128]{2,1,0:T(1,128)}), f32[32,1,128]{2,1,0:T(1,128)S(1)}, u32[]{:S(2)}, u32[]{:S(2)}) async-start(f32[32,1,128]{2,1,0:T(1,128)} %last_dots.1), calls=%async_computation.1 | async-start | bytes 32768 | tf_op jit(solution)/shard_map/all_to_all | solution.py:329
  (12 other events, 156.7 us)

commit v4 on v3

--- a/solution.py
+++ b/solution.py
@@ -33,53 +33,60 @@
     return lax.ppermute(block, "ep", [(i, i ^ bits) for i in range(count)])
 
 
-def place_kernel(index, meta, rows, out):
+def place_kernel(index, *refs):
+    count = (len(refs) - 1) // 2
+    metas, parts, out = refs[:count], refs[count : 2 * count], refs[-1]
     expert, core = index[16], index[17]
-    tokens = meta.shape[2]
+    tokens = metas[0].shape[2]
+    slots = parts[0].shape[0]
     lower = lax.broadcasted_iota(jnp.int32, (tokens, tokens), 0) > lax.broadcasted_iota(
         jnp.int32, (tokens, tokens), 1
     )
     lower = lower.astype(jnp.float32).astype(jnp.bfloat16)
-    slots = rows.shape[0]
     lane = lax.broadcasted_iota(jnp.int32, (tokens, slots), 1).astype(jnp.float32)
     wanted = expert.astype(jnp.float32)
-    for half in range(2):
-        owner = core if half == 0 else 1 - core
-        table = jnp.transpose(meta[owner])
-        first = table[:, 0:1] == wanted
-        second = table[:, 1:2] == wanted
-        named = jnp.where(first | second, 1.0, 0.0)
-        gate = jnp.where(first, table[:, 2:3], 0.0) + jnp.where(second, table[:, 3:4], 0.0)
-        wide = jnp.broadcast_to(named, (tokens, slots))
-        before = jnp.dot(lower, wide.astype(jnp.bfloat16), preferred_element_type=jnp.float32)
-        place = before + (owner * CAP).astype(jnp.float32)
-        onehot = jnp.where(place == lane, wide, 0.0).astype(jnp.bfloat16)
-        picked = jnp.dot(onehot, rows[...], preferred_element_type=jnp.float32)
-        out[0, half * tokens : (half + 1) * tokens, :] = (gate * picked).astype(out.dtype)
-
-
-def place_rows(index, meta, hidden, start, stop):
+    for chip in range(count):
+        for half in range(2):
+            owner = core if half == 0 else 1 - core
+            table = jnp.transpose(metas[chip][owner])
+            first = table[:, 0:1] == wanted
+            second = table[:, 1:2] == wanted
+            named = jnp.where(first | second, 1.0, 0.0)
+            gate = jnp.where(first, table[:, 2:3], 0.0) + jnp.where(second, table[:, 3:4], 0.0)
+            wide = jnp.broadcast_to(named, (tokens, slots))
+            before = jnp.dot(lower, wide.astype(jnp.bfloat16), preferred_element_type=jnp.float32)
+            place = before + (owner * CAP).astype(jnp.float32)
+            onehot = jnp.where(place == lane, wide, 0.0).astype(jnp.bfloat16)
+            picked = jnp.dot(onehot, parts[chip][...], preferred_element_type=jnp.float32)
+            out[chip, half * tokens : (half + 1) * tokens, :] = (gate * picked).astype(out.dtype)
+
+
+def place_rows(index, meta, hidden):
     tokens = meta.shape[2]
     units = hidden.shape[1]
-    count = stop - start
+    chips = 4
+
+    def meta_spec(k):
+        return pl.BlockSpec((2, 8, tokens), lambda i, ix: (ix[chips * i + k], 0, 0))
+
+    def part_spec(k):
+        return pl.BlockSpec((2 * CAP, units), lambda i, ix: (ix[18 + chips * i + k], 0))
+
     return pl.pallas_call(
         place_kernel,
         grid_spec=pltpu.PrefetchScalarGridSpec(
             num_scalar_prefetch=1,
-            grid=(count,),
-            in_specs=[
-                pl.BlockSpec((2, 8, tokens), lambda i, ix: (ix[start + i], 0, 0)),
-                pl.BlockSpec((2 * CAP, units), lambda i, ix: (ix[18 + start + i], 0)),
-            ],
-            out_specs=pl.BlockSpec((1, 2 * tokens, units), lambda i, ix: (i, 0, 0)),
-        ),
-        out_shape=jax.ShapeDtypeStruct((count, 2 * tokens, units), jnp.bfloat16),
-        cost_estimate=pl.CostEstimate(
-            flops=2 * count * 256 * 240 * (units + 128), bytes_accessed=count * 512 * units * 2, transcendentals=0
+            grid=(16 // chips,),
+            in_specs=[meta_spec(k) for k in range(chips)] + [part_spec(k) for k in range(chips)],
+            out_specs=pl.BlockSpec((chips, 2 * tokens, units), lambda i, ix: (i, 0, 0)),
+        ),
+        out_shape=jax.ShapeDtypeStruct((16, 2 * tokens, units), jnp.bfloat16),
+        cost_estimate=pl.CostEstimate(
+            flops=2 * 16 * 256 * 240 * (units + 128), bytes_accessed=16 * 512 * units * 2, transcendentals=0
         ),
         compiler_params=pltpu.CompilerParams(vmem_limit_bytes=VMEM_BYTES),
         name="place_rows",
-    )(index, meta, hidden)
+    )(index, *([meta] * chips), *([hidden] * chips))
 
 
 def block_dots(index, start, rows, hidden, weight, dots):
@@ -306,7 +313,7 @@
     hidden = jnp.concatenate([own_hidden, core_hidden, chip_hidden, far_hidden], axis=0)
     d2 = step(d1, 2)
     s2 = step(s1, 2, meta)
-    placed = place_rows(index, meta, hidden, 0, 16)
+    placed = place_rows(index, meta, hidden)
     d3 = step(d2, 2, placed)
     grads, dots = round_at(0, [same, *d1, *s1], None, None)
     s3 = step(s2, 2)

time: 220 us -> 220 us (level)
  transfers between devices with their start and end apart: 23 -> 23, of which waited for: 6 -> 7; matrix products, arithmetic and copies ran while one was open for 3% -> 3% of each run, Pallas kernels for 15% -> 14%
where the time goes in v4:
time: 220 us; the launch traced here: 219 us
  starting transfers between devices  109 us (50%)
  waiting for transfers between devices  62.5 us (28%)
  Pallas kernels  32.7 us (15%)
  local copies, waits for them, and re-layouts  7.57 us (3%)
  other arithmetic  5.81 us (3%)
    ppermute x16, starting transfers between devices, send_chips(): lax.ppermute(block, 'ep', [(i, (i + 2 * hops) % count) for i in range(cou...  64.3 us
    ppermute x16, waiting for transfers between devices, send_chips(): lax.ppermute(block, 'ep', [(i, (i + 2 * hops) % count) for i in range(cou...  56.9 us
    ppermute x4, starting transfers between devices, swap_bits(): return lax.ppermute(block, 'ep', [(i, i ^ bits) for i in range(count)])  17.3 us
    pallas_call x3, Pallas kernels, round_call(): pl.pallas_call(kernel, grid_spec=pltpu.PrefetchScalarGridSpec(num_scalar_...  12.9 us
    all_to_all x1, starting transfers between devices, shards(): meta = lax.all_to_all(meta, 'ep', split_axis=0, concat_axis=0, tiled=True)  11.4 us
    pallas_call x1, Pallas kernels, place_rows(): pl.pallas_call(place_kernel, grid_spec=pltpu.PrefetchScalarGridSpec(num_s...  11.1 us
    all_to_all x1, starting transfers between devices, shards(): lax.all_to_all(dots, 'ep', split_axis=0, concat_axis=0, tiled=True)  9.5 us
    ppermute x1, starting transfers between devices, shards(): lax.ppermute(moving, 'pp', [(i, rank_count - 1 - i) for i in range(rank_c...  6.83 us
  transfers between devices with their start and end apart: 23, of which 7 were waited for; matrix products, arithmetic and copies ran while one was open for 3% of the time, Pallas kernels for 14%

profile of v4, /device:TPU:1, one launch (start us, length us, event | category | flops | bytes accessed | tf_op | source)
XLA Modules:
  0.0 219.0 jit_solution(4750016467978527363)
XLA Ops:
  0.6 4.4 %collective-permute-start.1 = (bf16[960,512]{1,0:T(8,128)(2,1)}, bf16[960,512]{1,0:T(8,128)(2,1)}, u32[]{:S(2)}, u32[]{:S(2)}) collective-permute-start(bf16[960,512]{1,0:T(8,128)(2,1)} %bitcast.37), channel_id=1, source_target_pairs={{0,2},{1,3},{2,0},{3,1},{4,6},{5,7},{6,4},{7,5},{8,10},{9,11},{10,... | collective-permute-start | bytes 2949128 | tf_op jit(solution)/shard_map/ppermute | solution.py:33
  5.0 6.3 %collective-permute-start.2 = (bf16[960,512]{1,0:T(8,128)(2,1)}, bf16[960,512]{1,0:T(8,128)(2,1)}, u32[]{:S(2)}, u32[]{:S(2)}) collective-permute-start(bf16[960,512]{1,0:T(8,128)(2,1)} %bitcast.38), channel_id=1, source_target_pairs={{0,1},{1,0},{2,3},{3,2},{4,5},{5,4},{6,7},{7,6},{8,9},{9,8},{10,11... | collective-permute-start | bytes 2949128 | tf_op jit(solution)/shard_map/ppermute | solution.py:33
  16.8 11.4 %all-to-all-start = ((f32[32,8,128]{2,1,0:T(8,128)}), f32[32,8,128]{2,1,0:T(8,128)S(1)}, u32[]{:S(2)}, u32[]{:S(2)}) async-start(f32[32,8,128]{2,1,0:T(8,128)} %broadcast_in_dim.32), calls=%async_computation | async-start | bytes 262144 | tf_op jit(solution)/shard_map/all_to_all | solution.py:299
  28.4 4.2 %collective-permute-start.12 = (bf16[256,896]{1,0:T(8,128)(2,1)S(1)}, bf16[256,896]{1,0:T(8,128)(2,1)S(1)}, u32[]{:S(2)}, u32[]{:S(2)}) collective-permute-start(bf16[256,896]{1,0:T(8,128)(2,1)S(1)} %get-tuple-element.28.refs_0_), channel_id=1, source_target_pairs={{0,4},{1,5},{2,6},{3,7},{4,8},{5,9},{6,10},{7,11},{8,12},{9,13},{1... | collective-permute-start | bytes 1376264 | tf_op jit(solution)/shard_map/ppermute | solution.py:28
  32.6 11.2 %collective-permute-start.13 = (bf16[256,896]{1,0:T(8,128)(2,1)S(1)}, bf16[256,896]{1,0:T(8,128)(2,1)S(1)}, u32[]{:S(2)}, u32[]{:S(2)}) collective-permute-start(bf16[256,896]{1,0:T(8,128)(2,1)S(1)} %get-tuple-element.28.refs_0_), channel_id=1, source_target_pairs={{0,28},{1,29},{2,30},{3,31},{4,0},{5,1},{6,2},{7,3},{8,4},{9,5},{1... | collective-permute-start | bytes 1376264 | tf_op jit(solution)/shard_map/ppermute | solution.py:28
  43.7 4.6 %collective-permute-start.3 = (bf16[960,512]{1,0:T(8,128)(2,1)}, bf16[960,512]{1,0:T(8,128)(2,1)}, u32[]{:S(2)}, u32[]{:S(2)}) collective-permute-start(bf16[960,512]{1,0:T(8,128)(2,1)} %collective-permute-done.1), channel_id=1, source_target_pairs={{0,1},{1,0},{2,3},{3,2},{4,5},{5,4},{6,7},{7,6},{8,9},{9,8},{10,11... | collective-permute-start | bytes 2949128 | tf_op jit(solution)/shard_map/ppermute | solution.py:33
  50.3 4.6 %collective-permute-start.6 = (bf16[256,896]{1,0:T(8,128)(2,1)S(1)}, bf16[256,896]{1,0:T(8,128)(2,1)S(1)}, u32[]{:S(2)}, u32[]{:S(2)}) collective-permute-start(bf16[256,896]{1,0:T(8,128)(2,1)S(1)} %get-tuple-element.25), channel_id=1, source_target_pairs={{0,30},{1,31},{2,0},{3,1},{4,2},{5,3},{6,4},{7,5},{8,6},{9,7},{10,... | collective-permute-start | bytes 1376264 | tf_op jit(solution)/shard_map/ppermute | solution.py:28
  54.9 6.4 %collective-permute-done.12.refs_3_ = bf16[256,896]{1,0:T(8,128)(2,1)S(1)} collective-permute-done((bf16[256,896]{1,0:T(8,128)(2,1)S(1)}, bf16[256,896]{1,0:T(8,128)(2,1)S(1)}, u32[]{:S(2)}, u32[]{:S(2)}) %collective-permute-start.12) | collective-permute-done | bytes 458784 | tf_op jit(solution)/shard_map/ppermute | solution.py:28
  63.9 5.6 %collective-permute-start.17 = (bf16[256,896]{1,0:T(8,128)(2,1)S(1)}, bf16[256,896]{1,0:T(8,128)(2,1)}, u32[]{:S(2)}, u32[]{:S(2)}) collective-permute-start(bf16[256,896]{1,0:T(8,128)(2,1)S(1)} %collective-permute-done.13.refs_4_), channel_id=1, source_target_pairs={{0,28},{1,29},{2,30},{3,31},{4,0},{5,1},{6,2},{7,3},{8,4},{9,5},{1... | collective-permute-start | bytes 1376264 | tf_op jit(solution)/shard_map/ppermute | solution.py:28
  77.2 22.0 %collective-permute-done.14.refs_2_ = bf16[256,896]{1,0:T(8,128)(2,1)} collective-permute-done((bf16[256,896]{1,0:T(8,128)(2,1)S(1)}, bf16[256,896]{1,0:T(8,128)(2,1)}, u32[]{:S(2)}, u32[]{:S(2)}) %collective-permute-start.14) | collective-permute-done | bytes 458784 | tf_op jit(solution)/shard_map/ppermute | solution.py:28
  101.1 5.5 %collective-permute-start.18 = (bf16[256,896]{1,0:T(8,128)(2,1)}, bf16[256,896]{1,0:T(8,128)(2,1)S(1)}, u32[]{:S(2)}, u32[]{:S(2)}) collective-permute-start(bf16[256,896]{1,0:T(8,128)(2,1)} %collective-permute-done.17.refs_3_), channel_id=1, source_target_pairs={{0,28},{1,29},{2,30},{3,31},{4,0},{5,1},{6,2},{7,3},{8,4},{9,5},{1... | collective-permute-start | bytes 1376264 | tf_op jit(solution)/shard_map/ppermute | solution.py:28
  108.9 11.1 %place_rows.1 = bf16[16,256,512]{2,1,0:T(8,128)(2,1)S(1)} custom-call(s32[66]{0:T(128)S(1)} %concatenate.18.index.ix, f32[32,8,128]{2,1,0:T(8,128)S(1)} %all-to-all-done.refs_0_.refs_1_.refs_2_.refs_3_, f32[32,8,128]{2,1,0:T(8,128)S(1)} %all-to-all-done.refs_0_.refs_1_.refs_2_.refs_3_, f32[32,8,128]{2,1,0:T(8,128)S(1)} %all-to-all-done.refs_0_.refs_1_.refs_2_.refs_3_, ...), custom_call_target="tpu_custom_call" | custom-call | flops 1258291200 | bytes 8388608 | tf_op jit(solution)/shard_map/place_rows/pallas_call | solution.py:75
  124.3 3.4 %collective-permute-start.8 = (bf16[256,896]{1,0:T(8,128)(2,1)S(1)}, bf16[256,896]{1,0:T(8,128)(2,1)S(1)}, u32[]{:S(2)}, u32[]{:S(2)}) collective-permute-start(bf16[256,896]{1,0:T(8,128)(2,1)S(1)} %collective-permute-done.5.refs_0_), channel_id=1, source_target_pairs={{0,4},{1,5},{2,6},{3,7},{4,8},{5,9},{6,10},{7,11},{8,12},{9,13},{1... | collective-permute-start | bytes 1376264 | tf_op jit(solution)/shard_map/ppermute | solution.py:28
  130.7 4.0 %round_blocks.3 = (f32[512,896]{1,0:T(8,128)S(1)}, f32[32,1,128]{2,1,0:T(1,128)}) custom-call(s32[66]{0:T(128)S(1)} %concatenate.18.index.ix, bf16[5,256,512]{2,1,0:T(8,128)(2,1)S(1)} %slice.39.hid, bf16[512,896]{1,0:T(8,128)(2,1)S(1)} %bitcast.30, bf16[256,896]{1,0:T(8,128)(2,1)S(1)} %get-tuple-element.28.refs_0_, bf16[256,896]{1,0:T(8,128)(2,1)S(1)} %copy-done.9, ...), custom_call_target="tpu_custom_call" | custom-call | flops 2348810240 | bytes 7274496 | tf_op jit(solution)/shard_map/round_blocks/pallas_call | solution.py:139
  136.9 14.0 %collective-permute-done.10.refs_1_ = bf16[256,896]{1,0:T(8,128)(2,1)S(1)} collective-permute-done((bf16[256,896]{1,0:T(8,128)(2,1)S(1)}, bf16[256,896]{1,0:T(8,128)(2,1)S(1)}, u32[]{:S(2)}, u32[]{:S(2)}) %collective-permute-start.10) | collective-permute-done | bytes 458784 | tf_op jit(solution)/shard_map/ppermute | solution.py:28
  150.9 6.2 %collective-permute-start.11 = (bf16[256,896]{1,0:T(8,128)(2,1)S(1)}, bf16[256,896]{1,0:T(8,128)(2,1)S(1)}, u32[]{:S(2)}, u32[]{:S(2)}) collective-permute-start(bf16[256,896]{1,0:T(8,128)(2,1)S(1)} %collective-permute-done.10.refs_1_), channel_id=1, source_target_pairs={{0,28},{1,29},{2,30},{3,31},{4,0},{5,1},{6,2},{7,3},{8,4},{9,5},{1... | collective-permute-start | bytes 1376264 | tf_op jit(solution)/shard_map/ppermute | solution.py:28
  159.0 4.7 %round_blocks.4 = (f32[512,896]{1,0:T(8,128)S(1)}, f32[32,1,128]{2,1,0:T(1,128)}) custom-call(s32[66]{0:T(128)S(1)} %concatenate.18.index.ix, bf16[4,256,512]{2,1,0:T(8,128)(2,1)S(1)} %get-tuple-element.44.hid, bf16[512,896]{1,0:T(8,128)(2,1)S(1)} %bitcast.31, ...), custom_call_target="tpu_custom_call", output_to_operand_aliasing={{0}: (7, {}), {1}: (8, {})} | custom-call | flops 1879048192 | bytes 6553600 | tf_op jit(solution)/shard_map/round_blocks/pallas_call | solution.py:139
  163.8 5.5 %collective-permute-start.19 = (bf16[128,896]{1,0:T(8,128)(2,1)S(1)}, bf16[128,896]{1,0:T(8,128)(2,1)S(1)}, u32[]{:S(2)}, u32[]{:S(2)}) collective-permute-start(bf16[128,896]{1,0:T(8,128)(2,1)S(1)} %slice.36), channel_id=1, source_target_pairs={{0,28},{1,29},{2,30},{3,31},{4,0},{5,1},{6,2},{7,3},{8,4},{9,5},{1... | collective-permute-start | bytes 688136 | tf_op jit(solution)/shard_map/ppermute | solution.py:28
  169.3 4.2 %round_blocks.5 = (f32[512,896]{1,0:T(8,128)S(1)}, f32[32,1,128]{2,1,0:T(1,128)}) custom-call(s32[66]{0:T(128)S(1)} %concatenate.18.index.ix, bf16[4,256,512]{2,1,0:T(8,128)(2,1)S(1)} %get-tuple-element.45.hid, bf16[512,896]{1,0:T(8,128)(2,1)S(1)} %bitcast.32, ...), custom_call_target="tpu_custom_call", output_to_operand_aliasing={{0}: (7, {}), {1}: (8, {})} | custom-call | flops 1879048192 | bytes 6553600 | tf_op jit(solution)/shard_map/round_blocks/pallas_call | solution.py:139
  173.5 11.0 %collective-permute-done.19 = bf16[128,896]{1,0:T(8,128)(2,1)S(1)} collective-permute-done((bf16[128,896]{1,0:T(8,128)(2,1)S(1)}, bf16[128,896]{1,0:T(8,128)(2,1)S(1)}, u32[]{:S(2)}, u32[]{:S(2)}) %collective-permute-start.19) | collective-permute-done | bytes 229408 | tf_op jit(solution)/shard_map/ppermute | solution.py:28
  185.9 6.8 %collective-permute-start.20 = (bf16[256,896]{1,0:T(8,128)(2,1)}, bf16[256,896]{1,0:T(8,128)(2,1)}, u32[]{:S(2)}, u32[]{:S(2)}) collective-permute-start(bf16[256,896]{1,0:T(8,128)(2,1)} %last_grads.2), channel_id=1, source_target_pairs={{0,480},{32,448},{64,416},{96,384},{128,352},{160,320},{192,288},{... | collective-permute-start | bytes 1376264 | tf_op jit(solution)/shard_map/ppermute | solution.py:334
  195.8 9.5 %all-to-all-start.1 = ((f32[32,1,128]{2,1,0:T(1,128)}), f32[32,1,128]{2,1,0:T(1,128)S(1)}, u32[]{:S(2)}, u32[]{:S(2)}) async-start(f32[32,1,128]{2,1,0:T(1,128)} %last_dots.1), calls=%async_computation.1 | async-start | bytes 32768 | tf_op jit(solution)/shard_map/all_to_all | solution.py:336
  207.8 3.7 %adam_step.1 = (bf16[256,896]{1,0:T(8,128)(2,1)}, bf16[256,896]{1,0:T(8,128)(2,1)}, bf16[256,896]{1,0:T(8,128)(2,1)}) custom-call(s32[1]{0:T(128)} %bitcast.12.ix.which, bf16[256,896]{1,0:T(8,128)(2,1)S(1)} %last_grads.3.kept, bf16[256,896]{1,0:T(8,128)(2,1)} %collective-permute-done.20.received, bf16[512,896]{1,0:T(8,128)(2,1)S(1)} %bitcast.34, ...), custom_call_target="tpu_custom_call" | custom-call | flops 6881280 | bytes 3670016 | tf_op jit(solution)/shard_map/adam_step/pallas_call | solution.py:245
  211.4 5.6 %all-to-all-done.1 = f32[32,1,128]{2,1,0:T(1,128)S(1)} async-done(((f32[32,1,128]{2,1,0:T(1,128)}), f32[32,1,128]{2,1,0:T(1,128)S(1)}, u32[]{:S(2)}, u32[]{:S(2)}) %all-to-all-start.1) | async-done | bytes 16416 | tf_op jit(solution)/shard_map/all_to_all | solution.py:336
  (81 shorter events, 42.1 us)
Async XLA Ops:
  0.6 47.8 %copy-start.12 = (s32[16]{0:T(128)S(1)}, s32[16]{0:T(128)}, u32[]{:S(2)}) copy-start(s32[16]{0:T(128)} %constant.101.clone) | copy-start | bytes 196
  0.6 27.7 %collective-permute-start.1 = (bf16[960,512]{1,0:T(8,128)(2,1)}, bf16[960,512]{1,0:T(8,128)(2,1)}, u32[]{:S(2)}, u32[]{:S(2)}) collective-permute-start(bf16[960,512]{1,0:T(8,128)(2,1)} %bitcast.37), channel_id=1, source_target_pairs={{0,2},{1,3},{2,0},{3,1},{4,6},{5,7},{6,4},{7,5},{8,10},{9,11},{10,... | collective-permute-start | bytes 2949128 | tf_op jit(solution)/shard_map/ppermute | solution.py:33
  5.0 23.3 %collective-permute-start.2 = (bf16[960,512]{1,0:T(8,128)(2,1)}, bf16[960,512]{1,0:T(8,128)(2,1)}, u32[]{:S(2)}, u32[]{:S(2)}) collective-permute-start(bf16[960,512]{1,0:T(8,128)(2,1)} %bitcast.38), channel_id=1, source_target_pairs={{0,1},{1,0},{2,3},{3,2},{4,5},{5,4},{6,7},{7,6},{8,9},{9,8},{10,11... | collective-permute-start | bytes 2949128 | tf_op jit(solution)/shard_map/ppermute | solution.py:33
  12.8 15.4 %collective-permute-start = (bf16[2,128,896]{2,1,0:T(8,128)(2,1)S(1)}, bf16[2,128,896]{2,1,0:T(8,128)(2,1)S(1)}, u32[]{:S(2)}, u32[]{:S(2)}) collective-permute-start(bf16[2,128,896]{2,1,0:T(8,128)(2,1)S(1)} %pad_maximum_fusion.1), channel_id=1, source_target_pairs={{0,1},{1,0},{2,3},{3,2},{4,5},{5,4},{6,7},{7,6},{8,9},{9,8},{10,11... | collective-permute-start | bytes 1376264 | tf_op jit(solution)/shard_map/ppermute | solution.py:33
  16.8 38.1 %all-to-all-start = ((f32[32,8,128]{2,1,0:T(8,128)}), f32[32,8,128]{2,1,0:T(8,128)S(1)}, u32[]{:S(2)}, u32[]{:S(2)}) async-start(f32[32,8,128]{2,1,0:T(8,128)} %broadcast_in_dim.32), calls=%async_computation | async-start | bytes 262144 | tf_op jit(solution)/shard_map/all_to_all | solution.py:299
  28.4 33.0 %collective-permute-start.12 = (bf16[256,896]{1,0:T(8,128)(2,1)S(1)}, bf16[256,896]{1,0:T(8,128)(2,1)S(1)}, u32[]{:S(2)}, u32[]{:S(2)}) collective-permute-start(bf16[256,896]{1,0:T(8,128)(2,1)S(1)} %get-tuple-element.28.refs_0_), channel_id=1, source_target_pairs={{0,4},{1,5},{2,6},{3,7},{4,8},{5,9},{6,10},{7,11},{8,12},{9,13},{1... | collective-permute-start | bytes 1376264 | tf_op jit(solution)/shard_map/ppermute | solution.py:28
  32.6 28.8 %collective-permute-start.13 = (bf16[256,896]{1,0:T(8,128)(2,1)S(1)}, bf16[256,896]{1,0:T(8,128)(2,1)S(1)}, u32[]{:S(2)}, u32[]{:S(2)}) collective-permute-start(bf16[256,896]{1,0:T(8,128)(2,1)S(1)} %get-tuple-element.28.refs_0_), channel_id=1, source_target_pairs={{0,28},{1,29},{2,30},{3,31},{4,0},{5,1},{6,2},{7,3},{8,4},{9,5},{1... | collective-permute-start | bytes 1376264 | tf_op jit(solution)/shard_map/ppermute | solution.py:28
  43.7 62.9 %collective-permute-start.3 = (bf16[960,512]{1,0:T(8,128)(2,1)}, bf16[960,512]{1,0:T(8,128)(2,1)}, u32[]{:S(2)}, u32[]{:S(2)}) collective-permute-start(bf16[960,512]{1,0:T(8,128)(2,1)} %collective-permute-done.1), channel_id=1, source_target_pairs={{0,1},{1,0},{2,3},{3,2},{4,5},{5,4},{6,7},{7,6},{8,9},{9,8},{10,11... | collective-permute-start | bytes 2949128 | tf_op jit(solution)/shard_map/ppermute | solution.py:33
  48.4 21.4 %collective-permute-start.4 = (bf16[256,896]{1,0:T(8,128)(2,1)S(1)}, bf16[256,896]{1,0:T(8,128)(2,1)S(1)}, u32[]{:S(2)}, u32[]{:S(2)}) collective-permute-start(bf16[256,896]{1,0:T(8,128)(2,1)S(1)} %get-tuple-element.25), channel_id=1, source_target_pairs={{0,2},{1,3},{2,4},{3,5},{4,6},{5,7},{6,8},{7,9},{8,10},{9,11},{10,... | collective-permute-start | bytes 1376264 | tf_op jit(solution)/shard_map/ppermute | solution.py:28
  50.3 23.6 %collective-permute-start.6 = (bf16[256,896]{1,0:T(8,128)(2,1)S(1)}, bf16[256,896]{1,0:T(8,128)(2,1)S(1)}, u32[]{:S(2)}, u32[]{:S(2)}) collective-permute-start(bf16[256,896]{1,0:T(8,128)(2,1)S(1)} %get-tuple-element.25), channel_id=1, source_target_pairs={{0,30},{1,31},{2,0},{3,1},{4,2},{5,3},{6,4},{7,5},{8,6},{9,7},{10,... | collective-permute-start | bytes 1376264 | tf_op jit(solution)/shard_map/ppermute | solution.py:28
  61.3 37.9 %collective-permute-start.14 = (bf16[256,896]{1,0:T(8,128)(2,1)S(1)}, bf16[256,896]{1,0:T(8,128)(2,1)}, u32[]{:S(2)}, u32[]{:S(2)}) collective-permute-start(bf16[256,896]{1,0:T(8,128)(2,1)S(1)} %collective-permute-done.12.refs_3_), channel_id=1, source_target_pairs={{0,4},{1,5},{2,6},{3,7},{4,8},{5,9},{6,10},{7,11},{8,12},{9,13},{1... | collective-permute-start | bytes 1376264 | tf_op jit(solution)/shard_map/ppermute | solution.py:28
  63.9 37.2 %collective-permute-start.17 = (bf16[256,896]{1,0:T(8,128)(2,1)S(1)}, bf16[256,896]{1,0:T(8,128)(2,1)}, u32[]{:S(2)}, u32[]{:S(2)}) collective-permute-start(bf16[256,896]{1,0:T(8,128)(2,1)S(1)} %collective-permute-done.13.refs_4_), channel_id=1, source_target_pairs={{0,28},{1,29},{2,30},{3,31},{4,0},{5,1},{6,2},{7,3},{8,4},{9,5},{1... | collective-permute-start | bytes 1376264 | tf_op jit(solution)/shard_map/ppermute | solution.py:28
  69.8 51.7 %collective-permute-start.5 = (bf16[256,896]{1,0:T(8,128)(2,1)S(1)}, bf16[256,896]{1,0:T(8,128)(2,1)S(1)}, u32[]{:S(2)}, u32[]{:S(2)}) collective-permute-start(bf16[256,896]{1,0:T(8,128)(2,1)S(1)} %collective-permute-done.4.refs_1_), channel_id=1, source_target_pairs={{0,4},{1,5},{2,6},{3,7},{4,8},{5,9},{6,10},{7,11},{8,12},{9,13},{1... | collective-permute-start | bytes 1376264 | tf_op jit(solution)/shard_map/ppermute | solution.py:28
  73.9 47.6 %collective-permute-start.7 = (bf16[256,896]{1,0:T(8,128)(2,1)S(1)}, bf16[256,896]{1,0:T(8,128)(2,1)S(1)}, u32[]{:S(2)}, u32[]{:S(2)}) collective-permute-start(bf16[256,896]{1,0:T(8,128)(2,1)S(1)} %collective-permute-done.6.refs_2_), channel_id=1, source_target_pairs={{0,28},{1,29},{2,30},{3,31},{4,0},{5,1},{6,2},{7,3},{8,4},{9,5},{1... | collective-permute-start | bytes 1376264 | tf_op jit(solution)/shard_map/ppermute | solution.py:28
  99.2 35.7 %collective-permute-start.15 = (bf16[256,896]{1,0:T(8,128)(2,1)}, bf16[256,896]{1,0:T(8,128)(2,1)S(1)}, u32[]{:S(2)}, u32[]{:S(2)}) collective-permute-start(bf16[256,896]{1,0:T(8,128)(2,1)} %collective-permute-done.14.refs_2_), channel_id=1, source_target_pairs={{0,4},{1,5},{2,6},{3,7},{4,8},{5,9},{6,10},{7,11},{8,12},{9,13},{1... | collective-permute-start | bytes 1376264 | tf_op jit(solution)/shard_map/ppermute | solution.py:28
  101.1 62.6 %collective-permute-start.18 = (bf16[256,896]{1,0:T(8,128)(2,1)}, bf16[256,896]{1,0:T(8,128)(2,1)S(1)}, u32[]{:S(2)}, u32[]{:S(2)}) collective-permute-start(bf16[256,896]{1,0:T(8,128)(2,1)} %collective-permute-done.17.refs_3_), channel_id=1, source_target_pairs={{0,28},{1,29},{2,30},{3,31},{4,0},{5,1},{6,2},{7,3},{8,4},{9,5},{1... | collective-permute-start | bytes 1376264 | tf_op jit(solution)/shard_map/ppermute | solution.py:28
  121.5 29.4 %collective-permute-start.10 = (bf16[256,896]{1,0:T(8,128)(2,1)S(1)}, bf16[256,896]{1,0:T(8,128)(2,1)S(1)}, u32[]{:S(2)}, u32[]{:S(2)}) collective-permute-start(bf16[256,896]{1,0:T(8,128)(2,1)S(1)} %collective-permute-done.7.refs_1_), channel_id=1, source_target_pairs={{0,28},{1,29},{2,30},{3,31},{4,0},{5,1},{6,2},{7,3},{8,4},{9,5},{1... | collective-permute-start | bytes 1376264 | tf_op jit(solution)/shard_map/ppermute | solution.py:28
  124.3 32.8 %collective-permute-start.8 = (bf16[256,896]{1,0:T(8,128)(2,1)S(1)}, bf16[256,896]{1,0:T(8,128)(2,1)S(1)}, u32[]{:S(2)}, u32[]{:S(2)}) collective-permute-start(bf16[256,896]{1,0:T(8,128)(2,1)S(1)} %collective-permute-done.5.refs_0_), channel_id=1, source_target_pairs={{0,4},{1,5},{2,6},{3,7},{4,8},{5,9},{6,10},{7,11},{8,12},{9,13},{1... | collective-permute-start | bytes 1376264 | tf_op jit(solution)/shard_map/ppermute | solution.py:28
  135.0 38.5 %collective-permute-start.16 = (bf16[128,896]{1,0:T(8,128)(2,1)S(1)}, bf16[128,896]{1,0:T(8,128)(2,1)S(1)}, u32[]{:S(2)}, u32[]{:S(2)}) collective-permute-start(bf16[128,896]{1,0:T(8,128)(2,1)S(1)} %slice.35), channel_id=1, source_target_pairs={{0,4},{1,5},{2,6},{3,7},{4,8},{5,9},{6,10},{7,11},{8,12},{9,13},{1... | collective-permute-start | bytes 688136 | tf_op jit(solution)/shard_map/ppermute | solution.py:28
  150.9 33.7 %collective-permute-start.11 = (bf16[256,896]{1,0:T(8,128)(2,1)S(1)}, bf16[256,896]{1,0:T(8,128)(2,1)S(1)}, u32[]{:S(2)}, u32[]{:S(2)}) collective-permute-start(bf16[256,896]{1,0:T(8,128)(2,1)S(1)} %collective-permute-done.10.refs_1_), channel_id=1, source_target_pairs={{0,28},{1,29},{2,30},{3,31},{4,0},{5,1},{6,2},{7,3},{8,4},{9,5},{1... | collective-permute-start | bytes 1376264 | tf_op jit(solution)/shard_map/ppermute | solution.py:28
  157.1 27.5 %collective-permute-start.9 = (bf16[256,896]{1,0:T(8,128)(2,1)S(1)}, bf16[256,896]{1,0:T(8,128)(2,1)S(1)}, u32[]{:S(2)}, u32[]{:S(2)}) collective-permute-start(bf16[256,896]{1,0:T(8,128)(2,1)S(1)} %collective-permute-done.8.refs_0_), channel_id=1, source_target_pairs={{0,4},{1,5},{2,6},{3,7},{4,8},{5,9},{6,10},{7,11},{8,12},{9,13},{1... | collective-permute-start | bytes 1376264 | tf_op jit(solution)/shard_map/ppermute | solution.py:28
  163.8 20.7 %collective-permute-start.19 = (bf16[128,896]{1,0:T(8,128)(2,1)S(1)}, bf16[128,896]{1,0:T(8,128)(2,1)S(1)}, u32[]{:S(2)}, u32[]{:S(2)}) collective-permute-start(bf16[128,896]{1,0:T(8,128)(2,1)S(1)} %slice.36), channel_id=1, source_target_pairs={{0,28},{1,29},{2,30},{3,31},{4,0},{5,1},{6,2},{7,3},{8,4},{9,5},{1... | collective-permute-start | bytes 688136 | tf_op jit(solution)/shard_map/ppermute | solution.py:28
  185.9 21.0 %collective-permute-start.20 = (bf16[256,896]{1,0:T(8,128)(2,1)}, bf16[256,896]{1,0:T(8,128)(2,1)}, u32[]{:S(2)}, u32[]{:S(2)}) collective-permute-start(bf16[256,896]{1,0:T(8,128)(2,1)} %last_grads.2), channel_id=1, source_target_pairs={{0,480},{32,448},{64,416},{96,384},{128,352},{160,320},{192,288},{... | collective-permute-start | bytes 1376264 | tf_op jit(solution)/shard_map/ppermute | solution.py:334
  195.8 21.2 %all-to-all-start.1 = ((f32[32,1,128]{2,1,0:T(1,128)}), f32[32,1,128]{2,1,0:T(1,128)S(1)}, u32[]{:S(2)}, u32[]{:S(2)}) async-start(f32[32,1,128]{2,1,0:T(1,128)} %last_dots.1), calls=%async_computation.1 | async-start | bytes 32768 | tf_op jit(solution)/shard_map/all_to_all | solution.py:336
  (12 other events, 156.7 us)
